TPU v7x, 512 devices: a whole 4x8x8 slice. The times are simulated.
512 devices in a mesh: node: 8 (over z_lo, x), wide: 64 (over z_hi, y, core).
Axes of the slice: x: 4, y: 8, z: 8 (z_hi: 4, z_lo: 2; z = z_hi * 2 + z_lo), core: 2. Of those that a mesh axis runs over, the one named last changes fastest.
Arguments:
- features: bfloat16 [6144, 2048], P(('node', 'wide')), may hold values from -0.078125 to 0.078125
- weight: bfloat16 [6144, 18432], P('node', 'wide'), may hold values from -6 to 6
- moment_one: float32 [6144, 18432], P('node', 'wide'), may hold values from -6 to 6
- moment_two: float32 [6144, 18432], P('node', 'wide'), may hold values from 0.05 to 1
- cotangent: bfloat16 [2048, 18432], P('node', 'wide'), may hold values from -10 to 10
- new_owner: int32 [8, 64, 24], P('node', 'wide'), may hold values from 0 to 63, as said below
- new_slot: int32 [8, 64, 24], P('node', 'wide'), may hold values from 0 to 27, as said below
Outputs:
- projected: bfloat16 [2048, 18432], P('node', 'wide')
- moved_weight: bfloat16 [8, 1792, 32, 288], P('node', 'wide')
- moved_first: float32 [8, 1792, 32, 288], P('node', 'wide')
- moved_second: float32 [8, 1792, 32, 288], P('node', 'wide')
Inputs may be any that keep to these rules, and one draw needn't show every extreme that they name: new_owner[n, w, b] is the wide index that takes tile b of device (n, w). Within one node group no device hands more than 1 tiles to one peer, and each device takes at most 28 tiles; half of the devices take exactly 28, the others 20. `new_slot`: the slots of the tiles that one device takes over are distinct.
All inputs are finite; a program needn't handle non-finite values.
Results may differ from a plain program's by a relative error of at most 0.001.
Values may be sent and summed in bfloat16 or wider, within the bound.
A program may use at most 128 MiB of HBM per device.

v0:
```python
import jax
import jax.numpy as jnp
from jax import lax
from jax.sharding import PartitionSpec as P

TILE = 32


rate = 0.02
bias_one = 1.0 - 0.9**10
bias_two = 1.0 - 0.999**10


def adam_update(grad, weight, first, second):
    g = grad.astype(jnp.float32)
    first_new = 0.9 * first + 0.1 * g
    second_new = 0.999 * second + 0.001 * g * g
    update = first_new / bias_one / (jnp.sqrt(second_new / bias_two) + 1e-08)
    weight_new = (weight.astype(jnp.float32) - rate * update).astype(jnp.bfloat16)
    return (weight_new, first_new, second_new)


def tile_up(block):
    rows = block.shape[0] // TILE
    return block.reshape(rows, TILE, block.shape[1])


def pack_tiles(tiles, position, total):
    empty = jnp.zeros((total, TILE, tiles.shape[2]), tiles.dtype)
    return empty.at[position].set(tiles)


def place_tiles(received, dest, capacity):
    empty = jnp.zeros((capacity + 1, TILE, received.shape[2]), received.dtype)
    return empty.at[dest].set(received)[:capacity][None]


def on_device(features, weight, moment_one, moment_two, cotangent, new_owner, new_slot):
    peers = lax.axis_size("wide")
    local_rows = lax.all_gather(features, "wide", axis=0, tiled=True)
    projected = lax.psum_scatter(
        lax.dot_general(
            local_rows, weight, (((0,), (0,)), ((), ())), preferred_element_type=jnp.float32
        ),
        "node",
        scatter_dimension=0,
        tiled=True,
    ).astype(jnp.bfloat16)
    gradient = jnp.dot(
        local_rows,
        lax.all_gather(cotangent, "node", axis=0, tiled=True),
        preferred_element_type=jnp.float32,
    ).astype(jnp.bfloat16)
    owners = new_owner.reshape(-1)
    slots = new_slot.reshape(-1)
    blocks = owners.shape[0]
    capacity = blocks + blocks // 6
    per_peer = (capacity + peers - 1) // peers
    total_slots = peers * per_peer
    onehot = (owners[:, None] == jnp.arange(peers, dtype=jnp.int32)[None, :]).astype(jnp.int32)
    earlier = jnp.sum((jnp.cumsum(onehot, axis=0) - onehot) * onehot, axis=1)
    position = owners * per_peer + earlier
    outbox_slots = jnp.full((total_slots,), capacity, jnp.int32).at[position].set(slots)
    sent = (
        lax.all_to_all(
            pack_tiles(tile_up(gradient), position, total_slots).astype(jnp.float32),
            "wide",
            split_axis=0,
            concat_axis=0,
            tiled=True,
        ).astype(jnp.bfloat16),
        lax.all_to_all(
            pack_tiles(tile_up(weight), position, total_slots).astype(jnp.float32),
            "wide",
            split_axis=0,
            concat_axis=0,
            tiled=True,
        ).astype(jnp.bfloat16),
        lax.all_to_all(
            pack_tiles(tile_up(moment_one), position, total_slots),
            "wide",
            split_axis=0,
            concat_axis=0,
            tiled=True,
        ),
        lax.all_to_all(
            pack_tiles(tile_up(moment_two), position, total_slots),
            "wide",
            split_axis=0,
            concat_axis=0,
            tiled=True,
        ),
        lax.all_to_all(outbox_slots, "wide", split_axis=0, concat_axis=0, tiled=True),
    )
    grad_in, weight_in, first_in, second_in, dest = sent
    weight_out, first_out, second_out = adam_update(grad_in, weight_in, first_in, second_in)
    moved_weight = place_tiles(weight_out, dest, capacity)
    moved_first = place_tiles(first_out, dest, capacity)
    moved_second = place_tiles(second_out, dest, capacity)
    return (projected, moved_weight, moved_first, moved_second)


def solution(mesh):
    placed = (
        P(("node", "wide"), None),
        P("node", "wide"),
        P("node", "wide"),
        P("node", "wide"),
        P("node", "wide"),
        P("node", "wide", None),
        P("node", "wide", None),
    )
    return jax.shard_map(
        on_device,
        mesh=mesh,
        in_specs=placed,
        out_specs=(
            P("node", "wide"),
            P("node", "wide", None, None),
            P("node", "wide", None, None),
            P("node", "wide", None, None),
        ),
        check_vma=False,
    )
```

profile of v0, /device:TPU:1, one launch (start us, length us, event | category | flops | bytes accessed | tf_op | source)
XLA Modules:
  0.0 461.5 jit_solution(5629946091790245418)
XLA Ops:
  7.2 0.7 fusion.2
  7.9 0.8 select_reduce_fusion
  8.8 0.7 fusion.3
  9.4 0.8 scatter_custom_fusion
  10.2 0.7 copy.24
  10.9 17.6 %all-to-all-start = ((s32[64,1,1]{2,1,0:T(1,128)}), s32[64,1,1]{2,1,0:T(1,128)S(1)}, u32[]{:S(2)}, u32[]{:S(2)}) async-start(s32[64,1,1]{2,1,0:T(1,128)} %copy.24), calls=%async_computation.1 | async-start | bytes 65536 | tf_op jit(solution)/shard_map/all_to_all | solution.py:93
  28.6 1.3 copy.25
  29.9 1.3 broadcast.59.clone
  31.2 4.5 scatter_fusion
  35.6 4.5 all-to-all-done
  40.2 8.2 %all-to-all-start.1 = ((bf16[64,32,288]{2,1,0:T(8,128)(2,1)}), bf16[64,32,288]{2,1,0:T(8,128)(2,1)S(1)}, u32[]{:S(2)}, u32[]{:S(2)}) async-start(bf16[64,32,288]{2,1,0:T(8,128)(2,1)} %scatter_fusion), calls=%async_computation.2 | async-start | bytes 3145728 | tf_op jit(solution)/shard_map/all_to_all | solution.py:72
  48.4 1.5 copy.26
  50.0 2.1 broadcast.60.clone
  52.0 5.2 %scatter_fusion.1 = f32[64,32,288]{2,1,0:T(8,128)} fusion(f32[64,32,288]{2,1,0:T(8,128)} %broadcast.60.clone, s32[24]{0:T(128)S(1)} %fusion.3, f32[24,32,288]{2,1,0:T(8,128)S(1)} %bitcast.30), kind=kCustom, calls=%fused_computation.2 | custom fusion | bytes 2654304 | tf_op jit(solution)/shard_map/scatter | solution.py:30
  57.2 31.5 %all-to-all-done.1 = bf16[64,32,288]{2,1,0:T(8,128)(2,1)S(1)} async-done(((bf16[64,32,288]{2,1,0:T(8,128)(2,1)}), bf16[64,32,288]{2,1,0:T(8,128)(2,1)S(1)}, u32[]{:S(2)}, u32[]{:S(2)}) %all-to-all-start.1) | async-done | bytes 1179680 | tf_op jit(solution)/shard_map/all_to_all | solution.py:72
  88.7 0.0 copy-start.3
  88.7 1.1 copy-done.3
  89.9 11.1 %all-to-all-start.2 = ((f32[64,32,288]{2,1,0:T(8,128)}), f32[64,32,288]{2,1,0:T(8,128)S(1)}, u32[]{:S(2)}, u32[]{:S(2)}) async-start(f32[64,32,288]{2,1,0:T(8,128)} %scatter_fusion.1), calls=%async_computation.3 | async-start | bytes 6291456 | tf_op jit(solution)/shard_map/all_to_all | solution.py:79
  100.9 0.0 all-gather.6.cloned.1.call-start
  101.0 0.7 all-gather.6.cloned.1.call-update
  101.7 2.6 copy.28
  104.2 2.1 broadcast.60.clone.1
  106.4 5.6 %scatter_fusion.3 = f32[64,32,288]{2,1,0:T(8,128)} fusion(f32[64,32,288]{2,1,0:T(8,128)} %broadcast.60.clone.1, s32[24]{0:T(128)S(1)} %fusion.3, f32[24,32,288]{2,1,0:T(8,128)} %bitcast.31), kind=kCustom, calls=%fused_computation.4 | custom fusion | bytes 2654304 | tf_op jit(solution)/shard_map/scatter | solution.py:30
  112.0 71.2 %all-to-all-done.2 = f32[64,32,288]{2,1,0:T(8,128)S(1)} async-done(((f32[64,32,288]{2,1,0:T(8,128)}), f32[64,32,288]{2,1,0:T(8,128)S(1)}, u32[]{:S(2)}, u32[]{:S(2)}) %all-to-all-start.2) | async-done | bytes 2359328 | tf_op jit(solution)/shard_map/all_to_all | solution.py:79
  183.2 0.0 copy-start
  183.2 27.3 %all-to-all-start.4 = ((f32[64,32,288]{2,1,0:T(8,128)}), f32[64,32,288]{2,1,0:T(8,128)}, u32[]{:S(2)}, u32[]{:S(2)}) async-start(f32[64,32,288]{2,1,0:T(8,128)} %scatter_fusion.3), calls=%async_computation.5 | async-start | bytes 6291456 | tf_op jit(solution)/shard_map/all_to_all | solution.py:86
  210.4 0.0 all-gather.4.cloned.1.call-start
  210.5 0.7 all-gather.4.cloned.1.call-update
  211.2 0.0 copy-done
  211.2 0.0 reduce-scatter.2.cloned.1.call-start
  211.2 100.9 %all-gather.6.cloned.1.call-done = bf16[64,12,2048]{2,1,0:T(8,128)(2,1)} async-done(((bf16[1,12,2048]{2,1,0:T(8,128)(2,1)}), bf16[64,12,2048]{2,1,0:T(8,128)(2,1)}) %all-gather.6.cloned.1.call-update) | async-done | bytes 3145744 | tf_op jit(solution)/shard_map/all_gather | solution.py:40
  312.1 4.7 %reshape.151 = bf16[768,2048]{1,0:T(8,128)(2,1)S(1)} reshape(bf16[64,12,2048]{2,1,0:T(8,128)(2,1)} %all-gather.6.cloned.1.call-done) | data formatting | bytes 6291456
  316.8 3.5 fusion.9
  320.3 0.0 reduce-scatter.2.cloned.1.call-update
  320.4 29.1 %all-gather.4.cloned.1.call-done = bf16[2048,288]{0,1:T(8,128)(2,1)} async-done(((bf16[256,288]{0,1:T(8,128)(2,1)}), bf16[2048,288]{0,1:T(8,128)(2,1)}) %all-gather.4.cloned.1.call-update) | async-done | bytes 1179664 | tf_op jit(solution)/shard_map/all_gather | solution.py:51
  349.5 3.2 convolution_convert_fusion
  352.6 2.1 copy.27
  354.7 0.0 copy-start.1
  354.7 1.3 broadcast.59.clone.1
  356.0 4.8 %scatter_fusion.2 = bf16[64,32,288]{2,1,0:T(8,128)(2,1)} fusion(bf16[64,32,288]{2,1,0:T(8,128)(2,1)} %broadcast.59.clone.1, s32[24]{0:T(128)S(1)} %fusion.3, bf16[24,32,288]{2,1,0:T(8,128)(2,1)} %bitcast.32), kind=kCustom, calls=%fused_computation.3 | custom fusion | bytes 1327200 | tf_op jit(solution)/shard_map/scatter | solution.py:30
  360.8 0.0 all-to-all-done.4
  360.8 17.5 %all-to-all-start.3 = ((bf16[64,32,288]{2,1,0:T(8,128)(2,1)}), bf16[64,32,288]{2,1,0:T(8,128)(2,1)}, u32[]{:S(2)}, u32[]{:S(2)}) async-start(bf16[64,32,288]{2,1,0:T(8,128)(2,1)} %scatter_fusion.2), calls=%async_computation.4 | async-start | bytes 3145728 | tf_op jit(solution)/shard_map/all_to_all | solution.py:65
  378.3 1.2 reduce
  379.5 40.1 %all-to-all-done.3 = bf16[64,32,288]{2,1,0:T(8,128)(2,1)} async-done(((bf16[64,32,288]{2,1,0:T(8,128)(2,1)}), bf16[64,32,288]{2,1,0:T(8,128)(2,1)}, u32[]{:S(2)}, u32[]{:S(2)}) %all-to-all-start.3) | async-done | bytes 1179680 | tf_op jit(solution)/shard_map/all_to_all | solution.py:65
  419.6 0.0 copy-done.1
  419.6 8.0 %subtract_convert_fusion = (bf16[64,32,288]{2,1,0:T(8,128)(2,1)}, f32[64,32,288]{2,1,0:T(8,128)}, f32[64,32,288]{2,1,0:T(8,128)}) fusion(bf16[64,32,288]{2,1,0:T(8,128)(2,1)} %copy-done.3, bf16[64,32,288]{2,1,0:T(8,128)(2,1)} %all-to-all-done.3, f32[64,32,288]{2,1,0:T(8,128)S(1)} %copy-done.1, f32[64,32,288]{2,1,0:T(8,128)} %all-to-all-done.4), kind=kLoop, calls=%fused_computation.12 | loop fusion | flops 9437184 | bytes 12976128 | tf_op jit(solution)/shard_map/convert_element_type | solution.py:19
  427.6 0.1 broadcast_in_dim.10
  427.7 6.5 %scatter_fusion.4 = bf16[29,32,288]{2,1,0:T(8,128)(2,1)S(1)} fusion(bf16[29,32,288]{2,1,0:T(8,128)(2,1)S(1)} %broadcast_in_dim.10, s32[64]{0:T(128)S(1)} %fusion.4, bf16[64,32,288]{2,1,0:T(8,128)(2,1)} %get-tuple-element.4), kind=kCustom, calls=%fused_computation.5 | custom fusion | bytes 3539200 | tf_op jit(solution)/shard_map/scatter | solution.py:35
  434.2 0.0 copy-start.2
  434.2 0.8 copy-done.2
  435.1 0.2 broadcast.61.clone
  435.2 7.1 %scatter_fusion.6 = f32[29,32,288]{2,1,0:T(8,128)S(1)} fusion(f32[29,32,288]{2,1,0:T(8,128)S(1)} %broadcast.61.clone, s32[64]{0:T(128)S(1)} %fusion.4, f32[64,32,288]{2,1,0:T(8,128)} %get-tuple-element.6), kind=kCustom, calls=%fused_computation.7 | custom fusion | bytes 7078144 | tf_op jit(solution)/shard_map/scatter | solution.py:35
  442.3 0.2 broadcast.61.clone.1
  442.5 7.1 %scatter_fusion.5 = f32[29,32,288]{2,1,0:T(8,128)S(1)} fusion(f32[29,32,288]{2,1,0:T(8,128)S(1)} %broadcast.61.clone.1, s32[64]{0:T(128)S(1)} %fusion.4, f32[64,32,288]{2,1,0:T(8,128)} %get-tuple-element.5), kind=kCustom, calls=%fused_computation.6 | custom fusion | bytes 7078144 | tf_op jit(solution)/shard_map/scatter | solution.py:35
  449.6 2.0 slice_bitcast_fusion.2
  451.6 1.7 slice_bitcast_fusion
  453.3 0.0 reduce-scatter.2.cloned.1.call-done
  453.3 1.6 convert_element_type.30
  (2 shorter events, 0.1 us)
Async XLA Ops:
  10.9 29.2 %all-to-all-start = ((s32[64,1,1]{2,1,0:T(1,128)}), s32[64,1,1]{2,1,0:T(1,128)S(1)}, u32[]{:S(2)}, u32[]{:S(2)}) async-start(s32[64,1,1]{2,1,0:T(1,128)} %copy.24), calls=%async_computation.1 | async-start | bytes 65536 | tf_op jit(solution)/shard_map/all_to_all | solution.py:93
  40.2 48.5 %all-to-all-start.1 = ((bf16[64,32,288]{2,1,0:T(8,128)(2,1)}), bf16[64,32,288]{2,1,0:T(8,128)(2,1)S(1)}, u32[]{:S(2)}, u32[]{:S(2)}) async-start(bf16[64,32,288]{2,1,0:T(8,128)(2,1)} %scatter_fusion), calls=%async_computation.2 | async-start | bytes 3145728 | tf_op jit(solution)/shard_map/all_to_all | solution.py:72
  88.7 1.1 copy-start.3
  89.9 93.3 %all-to-all-start.2 = ((f32[64,32,288]{2,1,0:T(8,128)}), f32[64,32,288]{2,1,0:T(8,128)S(1)}, u32[]{:S(2)}, u32[]{:S(2)}) async-start(f32[64,32,288]{2,1,0:T(8,128)} %scatter_fusion.1), calls=%async_computation.3 | async-start | bytes 6291456 | tf_op jit(solution)/shard_map/all_to_all | solution.py:79
  100.9 211.2 %all-gather.6.cloned.1.call-start = ((), (), s32[]{:S(2)}) async-start(), calls=%async_computation.8 | async-start | bytes 4259840 | tf_op jit(solution)/shard_map/all_gather | solution.py:40
  183.2 28.0 %copy-start = (f32[64,32,288]{2,1,0:T(8,128)}, f32[64,32,288]{2,1,0:T(8,128)S(1)}, u32[]{:S(2)}) copy-start(f32[64,32,288]{2,1,0:T(8,128)S(1)} %all-to-all-done.2) | copy-start | bytes 7077892
  183.2 177.6 %all-to-all-start.4 = ((f32[64,32,288]{2,1,0:T(8,128)}), f32[64,32,288]{2,1,0:T(8,128)}, u32[]{:S(2)}, u32[]{:S(2)}) async-start(f32[64,32,288]{2,1,0:T(8,128)} %scatter_fusion.3), calls=%async_computation.5 | async-start | bytes 6291456 | tf_op jit(solution)/shard_map/all_to_all | solution.py:86
  210.4 139.0 %all-gather.4.cloned.1.call-start = ((), (), s32[]{:S(2)}) async-start(), calls=%async_computation.7 | async-start | bytes 1327104 | tf_op jit(solution)/shard_map/all_gather | solution.py:51
  211.2 242.1 %reduce-scatter.2.cloned.1.call-start = ((), (), s32[]{:S(2)}) async-start(), calls=%async_computation.6 | async-start | bytes 2654208 | tf_op jit(solution)/shard_map/reduce_scatter | solution.py:41
  354.7 65.0 %copy-start.1 = (f32[64,32,288]{2,1,0:T(8,128)S(1)}, f32[64,32,288]{2,1,0:T(8,128)}, u32[]{:S(2)}) copy-start(f32[64,32,288]{2,1,0:T(8,128)} %copy-done) | copy-start | bytes 7077892
  360.8 58.8 %all-to-all-start.3 = ((bf16[64,32,288]{2,1,0:T(8,128)(2,1)}), bf16[64,32,288]{2,1,0:T(8,128)(2,1)}, u32[]{:S(2)}, u32[]{:S(2)}) async-start(bf16[64,32,288]{2,1,0:T(8,128)(2,1)} %scatter_fusion.2), calls=%async_computation.4 | async-start | bytes 3145728 | tf_op jit(solution)/shard_map/all_to_all | solution.py:65
  434.2 0.9 copy-start.2
Sparse Core Ops, SparseCore 0:
  105.1 206.9 all-gather.5
  314.1 35.2 all-gather.3
  352.3 82.2 reduce-scatter.1
where the time goes:
time: 464 us; the launch traced here: 461 us
  waiting for transfers between devices  279 us (60%)
  starting transfers between devices  81.8 us (18%)
  local copies, waits for them, and re-layouts  67.4 us (15%)
  between operations  13.9 us (3%)
  other arithmetic  13.1 us (3%)
  matrix products  6.64 us (1%)
    all_gather x1, waiting for transfers between devices, on_device(): local_rows = lax.all_gather(features, 'wide', axis=0, tiled=True)  101 us
    all_to_all x1, waiting for transfers between devices, on_device(): lax.all_to_all(pack_tiles(tile_up(moment_one), position, total_slots), 'w...  71.2 us
    all_to_all x1, waiting for transfers between devices, on_device(): lax.all_to_all(pack_tiles(tile_up(gradient), position, total_slots).astyp...  40.1 us
    all_to_all x1, waiting for transfers between devices, on_device(): lax.all_to_all(pack_tiles(tile_up(weight), position, total_slots).astype(...  31.5 us
    all_gather x1, waiting for transfers between devices, on_device(): lax.all_gather(cotangent, 'node', axis=0, tiled=True)  29.1 us
    all_to_all x1, starting transfers between devices, on_device(): lax.all_to_all(pack_tiles(tile_up(moment_two), position, total_slots), 'w...  27.3 us
    scatter x3, local copies, waits for them, and re-layouts, place_tiles(): return empty.at[dest].set(received)[:capacity][None]  20.7 us
    scatter x4, local copies, waits for them, and re-layouts, pack_tiles(): return empty.at[position].set(tiles)  20.1 us
  transfers between devices with their start and end apart: 8, of which 6 were waited for; matrix products, arithmetic and copies ran while one was open for 17% of the time, Pallas kernels for 0%

commit v1 on v0

v1 whole, which is shorter than its diff:
```python
import jax
import jax.numpy as jnp
from jax import lax
from jax.experimental import pallas as pl
from jax.experimental.pallas import tpu as pltpu
from jax.sharding import PartitionSpec as P

TILE = 32
NZ, NY, NC = 4, 8, 2
NX = 4
NN = 2 * NX
MESH = pl.DeviceIdType.MESH
ANY = pl.BlockSpec(memory_space=pl.ANY)
HBM = pl.BlockSpec(memory_space=pltpu.HBM)
VMEM = pl.BlockSpec(memory_space=pltpu.VMEM)
SMEM = pl.BlockSpec(memory_space=pltpu.SMEM)
DMA = pltpu.SemaphoreType.DMA

rate = 0.02
bias_one = 1.0 - 0.9**10
bias_two = 1.0 - 0.999**10

TOP = 32767.0
LEAST = 2.0**-100


def place_of(w):
    return w // (NY * NC), (w // NC) % NY, w % NC


def node_peers_of(n, w):
    x = lax.rem(n, NX)
    base = n - x
    return (lax.rem(n + NX, NN), w), [(base + lax.rem(x + k, NX), w) for k in range(1, NX)]


HEAD = 1024
KEEP = 1536


def gather_kernel(
    owner_ref, slot_ref, x_in, c_in, wt_in, onet_in, twot_in,
    a_ref, b_ref, t_ref, call_ref, w_ref, one_ref, two_ref,
    x_ref, wt_ref, onet_ref, twot_ref,
    zs, zr, rs, rr, ls, lr, ss, sr, bs, br, bzs, bzr, bss, bsr,
    ts, tr, tzs, tzr, tss, tsr, ns, nr, loc,
):
    n = lax.axis_index("node")
    w = lax.axis_index("wide")
    z, y, c = place_of(w)

    def wide(zz, yy, cc):
        return (n, (lax.rem(zz + NZ, NZ) * NY + lax.rem(yy + NY, NY)) * NC + cc)

    sibling = wide(z, y, 1 - c)
    y_peers = [wide(z, y + k, c) for k in range(1, NY)]
    right, left = y_peers[0], y_peers[-1]
    z_peers = [wide(z + k, y, c) for k in range(1, NZ)]
    partner, x_peers = node_peers_of(n, w)

    barrier = pltpu.get_barrier_semaphore()
    peers = [sibling, partner] + y_peers + z_peers + x_peers
    for peer in peers:
        pl.semaphore_signal(barrier, inc=1, device_id=peer, device_id_type=MESH)

    own = [
        pltpu.make_async_copy(src, dst, loc.at[i])
        for i, (src, dst) in enumerate((
            (x_in, x_ref), (c_in, call_ref.at[n]),
            (onet_in, onet_ref), (twot_in, twot_ref), (wt_in, wt_ref),
        ))
    ]
    for copy in own:
        copy.start()
    t_ref[z, y, c, 0:1, :owner_ref.shape[1]] = owner_ref[...]
    t_ref[z, y, c, 1:2, :slot_ref.shape[1]] = slot_ref[...]
    own[0].wait()

    rows = x_ref.shape[0]
    extra = (x_ref.shape[1] - KEEP)
    a_ref[z, y, c, :rows, :] = x_ref[:, :HEAD]
    b_ref[z, y, c, :rows, :] = x_ref[:, HEAD:KEEP]
    for k in range(HEAD // extra):
        a_ref[z, y, c, rows:, k * extra:(k + 1) * extra] = x_ref[4 * k:4 * k + 4, KEEP:]
    b_ref[z, y, c, rows:, :] = x_ref[rows - 4:, KEEP:]
    own[1].wait()

    pl.semaphore_wait(barrier, len(peers))

    def send(ref, s, r, peer):
        copy = pltpu.make_async_remote_copy(
            src_ref=ref, dst_ref=ref, send_sem=s, recv_sem=r,
            device_id=peer, device_id_type=MESH,
        )
        copy.start()
        return copy

    z_copies = [
        send(a_ref.at[z, y, c], zs.at[k], zr.at[k], z_peers[k]) for k in range(NZ - 1)
    ]
    b_copies = [
        send(b_ref.at[z, y, c], bs.at[k], br.at[k], y_peers[k]) for k in range(NY - 1)
    ]
    across = send(call_ref.at[n], ns.at[0], nr.at[0], partner)
    x_copies = [
        send(call_ref.at[n], ns.at[k + 1], nr.at[k + 1], x_peers[k]) for k in range(NX - 1)
    ]
    t_copies = [
        send(t_ref.at[z, y, c], ts.at[k], tr.at[k], y_peers[k]) for k in range(NY - 1)
    ]

    def block(k, yy):
        return a_ref.at[lax.rem(z + k, NZ), lax.rem(yy + NY, NY), c]

    half = NY // 2
    order = (0, NZ - 1, 1, 2)
    from_left, from_right, to_sib = {}, {}, []
    for s in range(half + 1):
        for i, k in enumerate(order):
            if s == 0:
                if k > 0:
                    z_copies[NZ - k - 1].wait_recv()
            else:
                if (s - 1, k) in from_left:
                    from_left[s - 1, k].wait_recv()
                if (s - 1, k) in from_right:
                    from_right[s - 1, k].wait_recv()
            if s < half:
                last = s == half - 1
                if not last or i % 2 == 0:
                    from_left[s, k] = send(block(k, y - s), rs.at[s, k], rr.at[s, k], right)
                if not last or i % 2 == 1:
                    from_right[s, k] = send(block(k, y + s), ls.at[s, k], lr.at[s, k], left)
        to_sib.append(send(a_ref.at[:, lax.rem(y - s + NY, NY), c], ss.at[2 * s], sr.at[2 * s], sibling))
        if 0 < s < half:
            to_sib.append(
                send(a_ref.at[:, lax.rem(y + s, NY), c], ss.at[2 * s - 1], sr.at[2 * s - 1], sibling)
            )
        if s == 0:
            for copy in b_copies:
                copy.wait_recv()
            bz = [
                send(b_ref.at[z, :, c], bzs.at[k], bzr.at[k], z_peers[k]) for k in range(NZ - 1)
            ]
            sib_b = [send(b_ref.at[z, :, c], bss.at[0], bsr.at[0], sibling)]
            own[2].wait()
            one_ref[...] = onet_ref[...].T
        if s == 1:
            across.wait_recv()
            other = call_ref.at[lax.rem(n + NX, NN)]
            x_copies += [
                send(other, ns.at[k + NX], nr.at[k + NX], x_peers[k]) for k in range(NX - 1)
            ]
            for copy in t_copies:
                copy.wait_recv()
            tz = [
                send(t_ref.at[z, :, c], tzs.at[k], tzr.at[k], z_peers[k]) for k in range(NZ - 1)
            ]
            sib_t = [send(t_ref.at[z, :, c], tss.at[0], tsr.at[0], sibling)]
            own[3].wait()
            two_ref[...] = twot_ref[...].T
        if s == 2:
            own[4].wait()
            w_ref[...] = wt_ref[...].T
    for k in (NZ - 1, 1, 2):
        at = lax.rem(z + k, NZ)
        bz[NZ - k - 1].wait_recv()
        sib_b.append(send(b_ref.at[at, :, c], bss.at[k], bsr.at[k], sibling))
        tz[NZ - k - 1].wait_recv()
        sib_t.append(send(t_ref.at[at, :, c], tss.at[k], tsr.at[k], sibling))

    for copy in z_copies + b_copies + t_copies + bz + tz + [across]:
        copy.wait_send()
    for copy in list(from_left.values()) + list(from_right.values()):
        copy.wait_send()
    for copy in to_sib + sib_b + sib_t + x_copies:
        copy.wait()


def gather(owners, slots, features, cotangent, wt, onet, twot):
    rows, tokens = features.shape
    cw, ct = cotangent.shape
    width, depth = wt.shape
    half = NY // 2
    pad = rows + rows // 3
    f32, bf16 = jnp.float32, jnp.bfloat16
    a, b, t, call, w, one, two = pl.pallas_call(
        gather_kernel,
        out_shape=(
            jax.ShapeDtypeStruct((NZ, NY, NC, pad, HEAD), bf16),
            jax.ShapeDtypeStruct((NZ, NY, NC, pad, KEEP - HEAD), bf16),
            jax.ShapeDtypeStruct((NZ, NY, NC, 8, 128), jnp.int32),
            jax.ShapeDtypeStruct((NN, cw, ct), bf16),
            jax.ShapeDtypeStruct((depth, width), bf16),
            jax.ShapeDtypeStruct((depth, width), f32),
            jax.ShapeDtypeStruct((depth, width), f32),
        ),
        in_specs=[VMEM] * 2 + [ANY] * 5,
        out_specs=(VMEM,) * 7,
        scratch_shapes=[
            pltpu.VMEM((rows, tokens), bf16),
            pltpu.VMEM((width, depth), bf16),
            pltpu.VMEM((width, depth), f32),
            pltpu.VMEM((width, depth), f32),
            DMA((NZ - 1,)), DMA((NZ - 1,)),
            DMA((half, NZ)), DMA((half, NZ)),
            DMA((half, NZ)), DMA((half, NZ)),
            DMA((NY + 1,)), DMA((NY + 1,)),
            DMA((NY - 1,)), DMA((NY - 1,)),
            DMA((NZ - 1,)), DMA((NZ - 1,)),
            DMA((NZ,)), DMA((NZ,)),
            DMA((NY - 1,)), DMA((NY - 1,)),
            DMA((NZ - 1,)), DMA((NZ - 1,)),
            DMA((NZ,)), DMA((NZ,)),
            DMA((NN - 1,)), DMA((NN - 1,)),
            DMA((5,)),
        ],
        compiler_params=pltpu.CompilerParams(
            collective_id=0, has_side_effects=True, vmem_limit_bytes=32 * 1024 * 1024
        ),
        name="gather_blocks",
    )(
        owners, slots,
        *(pltpu.with_memory_space_constraint(v, pltpu.HBM) for v in (features, cotangent, wt, onet, twot)),
    )
    many = NZ * NY * NC
    a, b, t = (v.reshape((many,) + v.shape[3:]) for v in (a, b, t))
    return a, b, t, call, w, one, two


def project_kernel(a_ref, b_ref, wt_ref, f_ref, own_ref, p1_ref, p2_ref, p3_ref):
    n = lax.axis_index("node")
    x, high = lax.rem(n, NX), n // NX
    blocks, pad, _ = a_ref.shape
    rows = pad * 3 // 4
    tokens = f_ref.shape[1] // NN
    extra = f_ref.shape[1] - KEEP

    def arrange(i, carry):
        at = pl.ds(pl.multiple_of(i * 4 * rows, 16), 4 * rows)
        a = a_ref[pl.ds(4 * i, 4)]
        b = b_ref[pl.ds(4 * i, 4)]
        f_ref[at, :HEAD] = jnp.concatenate([a[j, :rows] for j in range(4)], axis=0)
        f_ref[at, HEAD:KEEP] = jnp.concatenate([b[j, :rows] for j in range(4)], axis=0)
        ends = []
        for j in range(4):
            for k in range(HEAD // extra):
                ends.append(a[j, rows:, k * extra:(k + 1) * extra])
            ends.append(b[j, rows:])
        f_ref[at, KEEP:] = jnp.concatenate(ends, axis=0)
        return carry

    lax.fori_loop(0, blocks // 4, arrange, 0)

    for k, out in ((1, p1_ref), (2, p2_ref), (3, p3_ref), (0, own_ref)):
        for h in range(2):
            node = lax.rem(high + h, 2) * NX + lax.rem(x + k, NX)
            at = pl.ds(pl.multiple_of(node * tokens, tokens), tokens)
            out[h] = jnp.dot(wt_ref[...], f_ref[:, at], preferred_element_type=jnp.float32)


def project(a, b, wt):
    blocks, pad, _ = a.shape
    width, depth = wt.shape
    tokens = KEEP + (KEEP // 3)
    share = jax.ShapeDtypeStruct((2, width, tokens // NN), jnp.float32)
    return pl.pallas_call(
        project_kernel,
        out_shape=(jax.ShapeDtypeStruct((depth, tokens), jnp.bfloat16),) + (share,) * NX,
        in_specs=[VMEM] * 3,
        out_specs=(VMEM,) * (NX + 1),
        compiler_params=pltpu.CompilerParams(vmem_limit_bytes=32 * 1024 * 1024),
        name="arrange_and_project",
    )(a, b, wt)


def sum_shares(own, shares):
    def node(high, x):
        return (high % 2) * NX + x % NX

    came = [
        lax.ppermute(
            share, "node",
            [(node(h, x), node(h, x + k + 1)) for h in range(2) for x in range(NX)],
        )
        for k, share in enumerate(shares)
    ]
    away = own[1] + came[0][1] + came[1][1] + came[2][1]
    across = lax.ppermute(
        away, "node", [(node(h, x), node(h + 1, x)) for h in range(2) for x in range(NX)]
    )
    total = own[0] + came[0][0] + came[1][0] + came[2][0]
    return (total + across).astype(jnp.bfloat16)


def fixed_point(x):
    most = jnp.maximum(jnp.max(jnp.abs(x), axis=1, keepdims=True), LEAST)
    power = jnp.ceil(jnp.log2(most))
    q = jnp.round(x * (TOP * jnp.exp2(-power)))
    return jnp.clip(q, -TOP, TOP).astype(jnp.int32), power.astype(jnp.int32)


def code_of(x):
    a = jnp.abs(x)
    some = a >= 2.0**-126
    safe = jnp.where(some, a, 1.0)
    e = jnp.floor(jnp.log2(safe))
    code = jnp.round((e + 127.0) * 128.0 + (safe * jnp.exp2(-e) - 1.0) * 128.0)
    code = jnp.where(some, code, 0.0)
    return jnp.where(x < 0.0, -code, code).astype(jnp.int32)


def value_of(code):
    a = jnp.abs(code)
    e = lax.shift_right_logical(a, 7)
    m = lax.bitwise_and(a, 127)
    v = (1.0 + m.astype(jnp.float32) * (1.0 / 128.0)) * jnp.exp2(e.astype(jnp.float32) - 127.0)
    v = jnp.where(a == 0, 0.0, v)
    return jnp.where(code < 0, -v, v)


def update_kernel(
    owner_ref, f_ref, c_ref, w_ref, one_ref, two_ref, send_ref, grad, packed, sems
):
    width = w_ref.shape[1]
    full = width // 128 * 128
    rest = width - full
    tail = pl.ds(3 * full, 128)
    part = f_ref.shape[0] // 3

    def put(b):
        return pltpu.make_async_copy(packed.at[b], send_ref.at[owner_ref[b]], sems.at[b])

    def one_tile(b, carry):
        at = pl.ds(pl.multiple_of(b * TILE, TILE), TILE)
        g = grad[at, :]
        first = 0.9 * one_ref[at, :] + 0.1 * g
        second = 0.999 * two_ref[at, :] + 0.001 * g * g
        step = first * (rate / bias_one) / (jnp.sqrt(second * (1.0 / bias_two)) + 1e-08)
        weight = (w_ref[at, :].astype(jnp.float32) - step).astype(jnp.bfloat16)
        qf, pf = fixed_point(first)
        qs, ps = fixed_point(second)
        cw = code_of(weight.astype(jnp.float32))
        packed[b, :, 0:full] = qf[:, :full].astype(jnp.int16)
        packed[b, :, full:2 * full] = qs[:, :full].astype(jnp.int16)
        packed[b, :, 2 * full:3 * full] = cw[:, :full].astype(jnp.int16)
        lane = lax.broadcasted_iota(jnp.int32, (TILE, 128 - 3 * rest), 1)
        powers = jnp.where(lane == 0, pf, ps)
        end = jnp.concatenate([qf[:, full:], qs[:, full:], cw[:, full:], powers], axis=1)
        packed[b, :, tail] = end.astype(jnp.int16)
        put(b).start()
        return carry

    def some(i, carry):
        at = pl.ds(pl.multiple_of(i * part, part), part)
        g = jnp.zeros((part, width), jnp.float32)
        for k in range(c_ref.shape[0]):
            tokens = c_ref.shape[2]
            g += lax.dot_general(
                f_ref[at, k * tokens:(k + 1) * tokens], c_ref[k],
                (((1,), (1,)), ((), ())), preferred_element_type=jnp.float32,
            )
        grad[at, :] = g.astype(jnp.bfloat16).astype(jnp.float32)
        lax.fori_loop(i * (part // TILE), (i + 1) * (part // TILE), one_tile, 0)
        return carry

    lax.fori_loop(0, 3, some, 0)

    def finish(b, carry):
        put(b).wait()
        return carry

    lax.fori_loop(0, owner_ref.shape[0], finish, 0)


def update(owners, rows, cots, weight, one, two, peers):
    depth, width = weight.shape
    lanes = 3 * (width // 128 * 128) + 128
    blocks = depth // TILE
    return pl.pallas_call(
        update_kernel,
        out_shape=pltpu.HBM((peers, TILE, lanes), jnp.int16),
        in_specs=[SMEM] + [VMEM] * 5,
        out_specs=HBM,
        scratch_shapes=[
            pltpu.VMEM((depth, width), jnp.float32),
            pltpu.VMEM((blocks, TILE, lanes), jnp.int16),
            DMA((blocks,)),
        ],
        compiler_params=pltpu.CompilerParams(vmem_limit_bytes=32 * 1024 * 1024),
        name="gradient_and_update",
    )(owners, rows, cots, weight, one, two)


def place_kernel(slot_ref, got_ref, weight_ref, first_ref, second_ref):
    capacity, _, width = weight_ref.shape[1:]
    full = width // 128 * 128
    rest = width - full
    step = pl.program_id(0)
    some = got_ref.shape[0]

    @pl.when(step == 0)
    def _():
        for ref in (weight_ref, first_ref, second_ref):
            ref[...] = jnp.zeros_like(ref)

    def one(p, carry):
        slot = slot_ref[step * some + p]

        @pl.when(slot < capacity)
        def _():
            q = got_ref[p].astype(jnp.int32)
            end = q[:, 3 * full:]
            pf = jnp.exp2(end[:, 3 * rest:3 * rest + 1].astype(jnp.float32)) * (1.0 / TOP)
            ps = jnp.exp2(end[:, 3 * rest + 1:3 * rest + 2].astype(jnp.float32)) * (1.0 / TOP)
            first_ref[0, slot, :, :full] = q[:, :full].astype(jnp.float32) * pf
            first_ref[0, slot, :, full:] = end[:, :rest].astype(jnp.float32) * pf
            second_ref[0, slot, :, :full] = q[:, full:2 * full].astype(jnp.float32) * ps
            second_ref[0, slot, :, full:] = end[:, rest:2 * rest].astype(jnp.float32) * ps
            weight_ref[0, slot, :, :full] = value_of(q[:, 2 * full:3 * full]).astype(jnp.bfloat16)
            weight_ref[0, slot, :, full:] = value_of(end[:, 2 * rest:3 * rest]).astype(jnp.bfloat16)

        return carry

    lax.fori_loop(0, got_ref.shape[0], one, 0)


def place(slots, got, capacity, width):
    shape = (1, capacity, TILE, width)
    return pl.pallas_call(
        place_kernel,
        out_shape=(
            jax.ShapeDtypeStruct(shape, jnp.bfloat16),
            jax.ShapeDtypeStruct(shape, jnp.float32),
            jax.ShapeDtypeStruct(shape, jnp.float32),
        ),
        grid=(8,),
        in_specs=[SMEM, pl.BlockSpec((got.shape[0] // 8,) + got.shape[1:], lambda i: (i, 0, 0))],
        out_specs=(pl.BlockSpec(shape, lambda i: (0, 0, 0, 0)),) * 3,
        compiler_params=pltpu.CompilerParams(vmem_limit_bytes=40 * 1024 * 1024),
        name="place_tiles",
    )(slots, got)


def on_device(features, weight, moment_one, moment_two, cotangent, new_owner, new_slot):
    peers = lax.axis_size("wide")
    owners = new_owner.reshape(-1)
    blocks = owners.shape[0]
    capacity = blocks + blocks // 6
    width = weight.shape[1]
    a, b, tables, cots, weight_rows, one, two = gather(
        new_owner[0], new_slot[0], features, cotangent.T, weight.T, moment_one.T, moment_two.T
    )
    rows, own, *shares = project(a, b, weight.T)
    projected = sum_shares(own, shares).T
    outbox = update(owners, rows, cots, weight_rows, one, two, peers)
    mine = tables[:, 0, :blocks] == lax.axis_index("wide")
    dest = jnp.min(jnp.where(mine, tables[:, 1, :blocks], capacity), axis=1)
    inbox = lax.all_to_all(outbox, "wide", split_axis=0, concat_axis=0, tiled=True)
    moved = place(dest, inbox, capacity, width)
    return (projected,) + tuple(moved)


def solution(mesh):
    placed = (
        P(("node", "wide"), None),
        P("node", "wide"),
        P("node", "wide"),
        P("node", "wide"),
        P("node", "wide"),
        P("node", "wide", None),
        P("node", "wide", None),
    )
    return jax.shard_map(
        on_device,
        mesh=mesh,
        in_specs=placed,
        out_specs=(
            P("node", "wide"),
            P("node", "wide", None, None),
            P("node", "wide", None, None),
            P("node", "wide", None, None),
        ),
        check_vma=False,
    )
```

time: 464 us -> 183 us (0.39)
  the two profiles are of different devices: /device:TPU:1 before, /device:TPU:43 now
where the time goes in v1:
time: 183 us; the launch traced here: 182 us
  waiting for transfers between devices  99.3 us (54%)
  Pallas kernels  55.5 us (30%)
  starting transfers between devices  21.5 us (12%)
  other arithmetic  3.15 us (2%)
  local copies, waits for them, and re-layouts  2.09 us (1%)
    ppermute x1, waiting for transfers between devices, sum_shares(): lax.ppermute(away, 'node', [(node(h, x), node(h + 1, x)) for h in range(2...  49.9 us
    pallas_call x1, Pallas kernels, gather(): pl.pallas_call(gather_kernel, out_shape=(jax.ShapeDtypeStruct((NZ, NY, NC...  36.7 us
    all_to_all x1, waiting for transfers between devices, on_device(): lax.all_to_all(outbox, 'wide', split_axis=0, concat_axis=0, tiled=True)  26.5 us
    ppermute x3, waiting for transfers between devices, sum_shares(): lax.ppermute(share, 'node', [(node(h, x), node(h, x + k + 1)) for h in ra...  23 us
    all_to_all x1, starting transfers between devices, on_device(): lax.all_to_all(outbox, 'wide', split_axis=0, concat_axis=0, tiled=True)  9.62 us
    ppermute x3, starting transfers between devices, sum_shares(): lax.ppermute(share, 'node', [(node(h, x), node(h, x + k + 1)) for h in ra...  9.6 us
    pallas_call x1, Pallas kernels, place(): pl.pallas_call(place_kernel, out_shape=(jax.ShapeDtypeStruct(shape, jnp.b...  8.72 us
    pallas_call x1, Pallas kernels, update(): pl.pallas_call(update_kernel, out_shape=pltpu.HBM((peers, TILE, lanes), j...  8.35 us
  transfers between devices with their start and end apart: 5, of which 5 were waited for; matrix products, arithmetic and copies ran while one was open for 2% of the time, Pallas kernels for 0%

profile of v1, /device:TPU:43, one launch (start us, length us, event | category | flops | bytes accessed | tf_op | source)
XLA Modules:
  0.0 182.4 jit_solution(12586406626166465023)
XLA Ops:
  0.6 0.0 copy-start
  0.6 0.0 copy-start.1
  0.7 0.7 copy-done.1
  1.4 0.0 copy-start.2
  1.4 0.7 copy-done.2
  2.0 36.7 %gather_blocks.1 = (bf16[4,8,2,16,1024]{4,3,2,1,0:T(8,128)(2,1)S(1)}, bf16[4,8,2,16,512]{4,3,2,1,0:T(8,128)(2,1)S(1)}, s32[4,8,2,8,128]{4,3,2,1,0:T(8,128)S(1)},...) custom-call(s32[1,24]{1,0:T(1,128)S(1)} %bitcast.27, ...), custom_call_target="tpu_custom_call" | custom-call | tf_op jit(solution)/shard_map/gather_blocks/pallas_call | solution.py:187
  38.7 0.0 copy-done
  38.7 1.8 arrange_and_project.1
  40.5 8.4 %gradient_and_update.1 = s16[64,32,896]{2,1,0:T(8,128)(2,1)} custom-call(s32[24]{0:T(128)S(1)} %bitcast.28, bf16[768,2048]{1,0:T(8,128)(2,1)S(1)} %get-tuple-element.26.f_ref, bf16[8,288,256]{2,1,0:T(8,128)(2,1)S(1)} %get-tuple-element.27.c_ref, bf16[768,288]{1,0:T(8,128)(2,1)S(1)} %get-tuple-element.28.w_ref, f32[768,288]{1,0:T(8,128)S(1)} %get-tuple-element.29.one_ref, ...), custom_call_target="tpu_custom_call" | custom-call | tf_op jit(solution)/shard_map/gradient_and_update/pallas_call | solution.py:380
  48.8 9.6 %all-to-all-start = ((s16[64,32,896]{2,1,0:T(8,128)(2,1)}), s16[64,32,896]{2,1,0:T(8,128)(2,1)}, u32[]{:S(2)}, u32[]{:S(2)}) async-start(s16[64,32,896]{2,1,0:T(8,128)(2,1)} %gradient_and_update.1), calls=%async_computation | async-start | bytes 7340032 | tf_op jit(solution)/shard_map/all_to_all | solution.py:459
  58.5 2.6 %collective-permute-start.2 = (f32[2,288,256]{2,1,0:T(8,128)S(1)}, f32[2,288,256]{2,1,0:T(8,128)S(1)}, u32[]{:S(2)}, u32[]{:S(2)}) collective-permute-start(f32[2,288,256]{2,1,0:T(8,128)S(1)} %get-tuple-element.24), channel_id=1, source_target_pairs={{0,192},{64,0},{128,64},{192,128},{256,448},{320,256},{384,320},{4... | collective-permute-start | bytes 1769480 | tf_op jit(solution)/shard_map/ppermute | solution.py:282
  61.1 3.5 %collective-permute-start.1 = (f32[2,288,256]{2,1,0:T(8,128)S(1)}, f32[2,288,256]{2,1,0:T(8,128)S(1)}, u32[]{:S(2)}, u32[]{:S(2)}) collective-permute-start(f32[2,288,256]{2,1,0:T(8,128)S(1)} %get-tuple-element.23), channel_id=1, source_target_pairs={{0,128},{64,192},{128,0},{192,64},{256,384},{320,448},{384,256},{4... | collective-permute-start | bytes 1769480 | tf_op jit(solution)/shard_map/ppermute | solution.py:282
  64.6 3.4 %collective-permute-start = (f32[2,288,256]{2,1,0:T(8,128)S(1)}, f32[2,288,256]{2,1,0:T(8,128)S(1)}, u32[]{:S(2)}, u32[]{:S(2)}) collective-permute-start(f32[2,288,256]{2,1,0:T(8,128)S(1)} %get-tuple-element.22), channel_id=1, source_target_pairs={{0,64},{64,128},{128,192},{192,0},{256,320},{320,384},{384,448},{4... | collective-permute-start | bytes 1769480 | tf_op jit(solution)/shard_map/ppermute | solution.py:282
  68.1 6.9 %collective-permute-done.2 = f32[2,288,256]{2,1,0:T(8,128)S(1)} collective-permute-done((f32[2,288,256]{2,1,0:T(8,128)S(1)}, f32[2,288,256]{2,1,0:T(8,128)S(1)}, u32[]{:S(2)}, u32[]{:S(2)}) %collective-permute-start.2) | collective-permute-done | bytes 589856 | tf_op jit(solution)/shard_map/ppermute | solution.py:282
  75.0 13.5 %collective-permute-done.1 = f32[2,288,256]{2,1,0:T(8,128)S(1)} collective-permute-done((f32[2,288,256]{2,1,0:T(8,128)S(1)}, f32[2,288,256]{2,1,0:T(8,128)S(1)}, u32[]{:S(2)}, u32[]{:S(2)}) %collective-permute-start.1) | collective-permute-done | bytes 589856 | tf_op jit(solution)/shard_map/ppermute | solution.py:282
  88.5 0.0 copy-start.3
  88.5 2.5 %collective-permute-done = f32[2,288,256]{2,1,0:T(8,128)S(1)} collective-permute-done((f32[2,288,256]{2,1,0:T(8,128)S(1)}, f32[2,288,256]{2,1,0:T(8,128)S(1)}, u32[]{:S(2)}, u32[]{:S(2)}) %collective-permute-start) | collective-permute-done | bytes 589856 | tf_op jit(solution)/shard_map/ppermute | solution.py:282
  91.1 0.0 copy-start.4
  91.1 0.0 copy-done.3
  91.1 0.1 fusion
  91.2 0.7 copy-done.4
  91.9 2.3 %collective-permute-start.3 = (f32[288,256]{1,0:T(8,128)S(1)}, f32[288,256]{1,0:T(8,128)S(1)}, u32[]{:S(2)}, u32[]{:S(2)}) collective-permute-start(f32[288,256]{1,0:T(8,128)S(1)} %fusion), channel_id=1, source_target_pairs={{0,256},{64,320},{128,384},{192,448},{256,0},{320,64},{384,128},{4... | collective-permute-start | bytes 884744 | tf_op jit(solution)/shard_map/ppermute | solution.py:289
  94.2 1.3 fusion.5.slot_ref
  95.5 49.9 %collective-permute-done.3 = f32[288,256]{1,0:T(8,128)S(1)} collective-permute-done((f32[288,256]{1,0:T(8,128)S(1)}, f32[288,256]{1,0:T(8,128)S(1)}, u32[]{:S(2)}, u32[]{:S(2)}) %collective-permute-start.3) | collective-permute-done | bytes 294944 | tf_op jit(solution)/shard_map/ppermute | solution.py:289
  145.4 1.8 fusion.4
  147.2 26.5 %all-to-all-done.got_ref = s16[64,32,896]{2,1,0:T(8,128)(2,1)} async-done(((s16[64,32,896]{2,1,0:T(8,128)(2,1)}), s16[64,32,896]{2,1,0:T(8,128)(2,1)}, u32[]{:S(2)}, u32[]{:S(2)}) %all-to-all-start) | async-done | bytes 3670048 | tf_op jit(solution)/shard_map/all_to_all | solution.py:459
  173.7 8.7 %place_tiles.1 = (bf16[1,28,32,288]{3,2,1,0:T(8,128)(2,1)}, f32[1,28,32,288]{3,2,1,0:T(8,128)}, f32[1,28,32,288]{3,2,1,0:T(8,128)}) custom-call(s32[64]{0:T(128)S(1)} %fusion.5.slot_ref, s16[64,32,896]{2,1,0:T(8,128)(2,1)} %all-to-all-done.got_ref), custom_call_target="tpu_custom_call" | custom-call | tf_op jit(solution)/shard_map/place_tiles/pallas_call | solution.py:430
Async XLA Ops:
  0.6 38.1 %copy-start = (bf16[768,288]{0,1:T(8,128)(2,1)S(1)}, bf16[768,288]{0,1:T(8,128)(2,1)}, u32[]{:S(2)}) copy-start(bf16[768,288]{0,1:T(8,128)(2,1)} %param.8) | copy-start | bytes 1327108
  0.6 0.7 copy-start.1
  1.4 0.7 copy-start.2
  48.8 124.8 %all-to-all-start = ((s16[64,32,896]{2,1,0:T(8,128)(2,1)}), s16[64,32,896]{2,1,0:T(8,128)(2,1)}, u32[]{:S(2)}, u32[]{:S(2)}) async-start(s16[64,32,896]{2,1,0:T(8,128)(2,1)} %gradient_and_update.1), calls=%async_computation | async-start | bytes 7340032 | tf_op jit(solution)/shard_map/all_to_all | solution.py:459
  58.5 16.6 %collective-permute-start.2 = (f32[2,288,256]{2,1,0:T(8,128)S(1)}, f32[2,288,256]{2,1,0:T(8,128)S(1)}, u32[]{:S(2)}, u32[]{:S(2)}) collective-permute-start(f32[2,288,256]{2,1,0:T(8,128)S(1)} %get-tuple-element.24), channel_id=1, source_target_pairs={{0,192},{64,0},{128,64},{192,128},{256,448},{320,256},{384,320},{4... | collective-permute-start | bytes 1769480 | tf_op jit(solution)/shard_map/ppermute | solution.py:282
  61.1 27.4 %collective-permute-start.1 = (f32[2,288,256]{2,1,0:T(8,128)S(1)}, f32[2,288,256]{2,1,0:T(8,128)S(1)}, u32[]{:S(2)}, u32[]{:S(2)}) collective-permute-start(f32[2,288,256]{2,1,0:T(8,128)S(1)} %get-tuple-element.23), channel_id=1, source_target_pairs={{0,128},{64,192},{128,0},{192,64},{256,384},{320,448},{384,256},{4... | collective-permute-start | bytes 1769480 | tf_op jit(solution)/shard_map/ppermute | solution.py:282
  64.6 26.4 %collective-permute-start = (f32[2,288,256]{2,1,0:T(8,128)S(1)}, f32[2,288,256]{2,1,0:T(8,128)S(1)}, u32[]{:S(2)}, u32[]{:S(2)}) collective-permute-start(f32[2,288,256]{2,1,0:T(8,128)S(1)} %get-tuple-element.22), channel_id=1, source_target_pairs={{0,64},{64,128},{128,192},{192,0},{256,320},{320,384},{384,448},{4... | collective-permute-start | bytes 1769480 | tf_op jit(solution)/shard_map/ppermute | solution.py:282
  88.5 2.6 %copy-start.3 = (f32[2,288,256]{2,1,0:T(8,128)}, f32[2,288,256]{2,1,0:T(8,128)S(1)}, u32[]{:S(2)}) copy-start(f32[2,288,256]{2,1,0:T(8,128)S(1)} %collective-permute-done.1) | copy-start | bytes 1769476
  91.1 0.8 copy-start.4
  91.9 53.5 %collective-permute-start.3 = (f32[288,256]{1,0:T(8,128)S(1)}, f32[288,256]{1,0:T(8,128)S(1)}, u32[]{:S(2)}, u32[]{:S(2)}) collective-permute-start(f32[288,256]{1,0:T(8,128)S(1)} %fusion), channel_id=1, source_target_pairs={{0,256},{64,320},{128,384},{192,448},{256,0},{320,64},{384,128},{4... | collective-permute-start | bytes 884744 | tf_op jit(solution)/shard_map/ppermute | solution.py:289

commit v2 on v1

--- a/solution.py
+++ b/solution.py
@@ -274,25 +274,6 @@
     )(a, b, wt)
 
 
-def sum_shares(own, shares):
-    def node(high, x):
-        return (high % 2) * NX + x % NX
-
-    came = [
-        lax.ppermute(
-            share, "node",
-            [(node(h, x), node(h, x + k + 1)) for h in range(2) for x in range(NX)],
-        )
-        for k, share in enumerate(shares)
-    ]
-    away = own[1] + came[0][1] + came[1][1] + came[2][1]
-    across = lax.ppermute(
-        away, "node", [(node(h, x), node(h + 1, x)) for h in range(2) for x in range(NX)]
-    )
-    total = own[0] + came[0][0] + came[1][0] + came[2][0]
-    return (total + across).astype(jnp.bfloat16)
-
-
 def fixed_point(x):
     most = jnp.maximum(jnp.max(jnp.abs(x), axis=1, keepdims=True), LEAST)
     power = jnp.ceil(jnp.log2(most))
@@ -319,114 +300,202 @@
     return jnp.where(code < 0, -v, v)
 
 
-def update_kernel(
-    owner_ref, f_ref, c_ref, w_ref, one_ref, two_ref, send_ref, grad, packed, sems
+def exchange_kernel(
+    tile_ref, f_ref, c_ref, w_ref, one_ref, two_ref, own_ref, p1_ref, p2_ref, p3_ref,
+    inbox_ref, out_ref, grad, outbox, got, total, across_got,
+    send_sem, recv_sem, xs, xr, acs, acr, loc,
 ):
-    width = w_ref.shape[1]
+    n = lax.axis_index("node")
+    w = lax.axis_index("wide")
+    many = outbox.shape[0]
+    partner, x_peers = node_peers_of(n, w)
+    width = w_ref.shape[2]
     full = width // 128 * 128
     rest = width - full
-    tail = pl.ds(3 * full, 128)
-    part = f_ref.shape[0] // 3
-
-    def put(b):
-        return pltpu.make_async_copy(packed.at[b], send_ref.at[owner_ref[b]], sems.at[b])
-
-    def one_tile(b, carry):
-        at = pl.ds(pl.multiple_of(b * TILE, TILE), TILE)
-        g = grad[at, :]
-        first = 0.9 * one_ref[at, :] + 0.1 * g
-        second = 0.999 * two_ref[at, :] + 0.001 * g * g
-        step = first * (rate / bias_one) / (jnp.sqrt(second * (1.0 / bias_two)) + 1e-08)
-        weight = (w_ref[at, :].astype(jnp.float32) - step).astype(jnp.bfloat16)
-        qf, pf = fixed_point(first)
-        qs, ps = fixed_point(second)
-        cw = code_of(weight.astype(jnp.float32))
-        packed[b, :, 0:full] = qf[:, :full].astype(jnp.int16)
-        packed[b, :, full:2 * full] = qs[:, :full].astype(jnp.int16)
-        packed[b, :, 2 * full:3 * full] = cw[:, :full].astype(jnp.int16)
-        lane = lax.broadcasted_iota(jnp.int32, (TILE, 128 - 3 * rest), 1)
-        powers = jnp.where(lane == 0, pf, ps)
-        end = jnp.concatenate([qf[:, full:], qs[:, full:], cw[:, full:], powers], axis=1)
-        packed[b, :, tail] = end.astype(jnp.int16)
-        put(b).start()
+
+    def peer_of(i):
+        step = lax.rem(i * 27, many)
+        return lax.rem(w + step, many), step
+
+    barrier = pltpu.get_barrier_semaphore()
+    for peer in [partner] + x_peers:
+        pl.semaphore_signal(barrier, inc=1, device_id=peer, device_id_type=MESH)
+
+    def greet(i, carry):
+        p, _ = peer_of(i)
+        pl.semaphore_signal(barrier, inc=1, device_id=(n, p), device_id_type=MESH)
         return carry
 
-    def some(i, carry):
-        at = pl.ds(pl.multiple_of(i * part, part), part)
-        g = jnp.zeros((part, width), jnp.float32)
+    lax.fori_loop(1, many, greet, 0)
+
+    part = grad.shape[0] // 3
+    tokens = c_ref.shape[2]
+
+    def multiply(i, carry):
+        at = pl.ds(pl.multiple_of(i * part * TILE, 256), part * TILE)
+        g = jnp.zeros((part * TILE, width), jnp.float32)
         for k in range(c_ref.shape[0]):
-            tokens = c_ref.shape[2]
             g += lax.dot_general(
                 f_ref[at, k * tokens:(k + 1) * tokens], c_ref[k],
                 (((1,), (1,)), ((), ())), preferred_element_type=jnp.float32,
             )
-        grad[at, :] = g.astype(jnp.bfloat16).astype(jnp.float32)
-        lax.fori_loop(i * (part // TILE), (i + 1) * (part // TILE), one_tile, 0)
+        g = g.astype(jnp.bfloat16).astype(jnp.float32)
+        grad[pl.ds(i * part, part)] = g.reshape(part, TILE, width)
         return carry
 
-    lax.fori_loop(0, 3, some, 0)
-
-    def finish(b, carry):
-        put(b).wait()
+    lax.fori_loop(0, 3, multiply, 0)
+    pl.semaphore_wait(barrier, many - 1 + NX)
+
+    shares = (p1_ref, p2_ref, p3_ref)
+    x_copies = []
+    for k in range(NX - 1):
+        copy = pltpu.make_async_remote_copy(
+            src_ref=shares[k], dst_ref=got.at[k], send_sem=xs.at[k], recv_sem=xr.at[k],
+            device_id=x_peers[k], device_id_type=MESH,
+        )
+        copy.start()
+        x_copies.append(copy)
+
+    def pack(p):
+        b = tile_ref[p]
+        g = grad[b]
+        first = 0.9 * one_ref[b] + 0.1 * g
+        second = 0.999 * two_ref[b] + 0.001 * g * g
+        step = first * (rate / bias_one) / (jnp.sqrt(second * (1.0 / bias_two)) + 1e-08)
+        weight = (w_ref[b].astype(jnp.float32) - step).astype(jnp.bfloat16)
+        qf, pf = fixed_point(first)
+        qs, ps = fixed_point(second)
+        cw = code_of(weight.astype(jnp.float32))
+        outbox[p, :, 0:full] = qf[:, :full].astype(jnp.int16)
+        outbox[p, :, full:2 * full] = qs[:, :full].astype(jnp.int16)
+        outbox[p, :, 2 * full:3 * full] = cw[:, :full].astype(jnp.int16)
+        lane = lax.broadcasted_iota(jnp.int32, (TILE, 128 - 3 * rest), 1)
+        powers = jnp.where(lane == 0, pf, ps)
+        end = jnp.concatenate([qf[:, full:], qs[:, full:], cw[:, full:], powers], axis=1)
+        outbox[p, :, 3 * full:] = end.astype(jnp.int16)
+
+    def copy_to(p, step):
+        return pltpu.make_async_remote_copy(
+            src_ref=outbox.at[p], dst_ref=inbox_ref.at[w],
+            send_sem=send_sem.at[step], recv_sem=recv_sem.at[step],
+            device_id=(n, p), device_id_type=MESH,
+        )
+
+    def send(i, carry):
+        p, step = peer_of(i)
+        pack(p)
+        copy_to(p, step).start()
         return carry
 
-    lax.fori_loop(0, owner_ref.shape[0], finish, 0)
-
-
-def update(owners, rows, cots, weight, one, two, peers):
+    lax.fori_loop(1, many, send, 0)
+    pack(w)
+    mine = pltpu.make_async_copy(outbox.at[w], inbox_ref.at[w], loc)
+    mine.start()
+
+    for copy in x_copies:
+        copy.wait_recv()
+    total[...] = own_ref[1] + got[0, 1] + got[1, 1] + got[2, 1]
+    across = pltpu.make_async_remote_copy(
+        src_ref=total, dst_ref=across_got, send_sem=acs, recv_sem=acr,
+        device_id=partner, device_id_type=MESH,
+    )
+    across.start()
+    near = own_ref[0] + got[0, 0] + got[1, 0] + got[2, 0]
+    across.wait_recv()
+    out_ref[...] = (near + across_got[...]).astype(jnp.bfloat16)
+
+    def finish(i, carry):
+        p, step = peer_of(i)
+        copy_to(p, step).wait()
+        return carry
+
+    lax.fori_loop(1, many, finish, 0)
+    mine.wait()
+    across.wait_send()
+    for copy in x_copies:
+        copy.wait_send()
+
+
+def exchange(tile_of, rows, cots, weight, one, two, shares, peers):
     depth, width = weight.shape
     lanes = 3 * (width // 128 * 128) + 128
     blocks = depth // TILE
+    share = shares[0].shape
+    f32 = jnp.float32
+    weight, one, two = (v.reshape(blocks, TILE, width) for v in (weight, one, two))
     return pl.pallas_call(
-        update_kernel,
-        out_shape=pltpu.HBM((peers, TILE, lanes), jnp.int16),
-        in_specs=[SMEM] + [VMEM] * 5,
-        out_specs=HBM,
+        exchange_kernel,
+        out_shape=(
+            pltpu.HBM((peers, TILE, lanes), jnp.int16),
+            jax.ShapeDtypeStruct(share[1:], jnp.bfloat16),
+        ),
+        in_specs=[SMEM] + [VMEM] * 9,
+        out_specs=(HBM, VMEM),
         scratch_shapes=[
-            pltpu.VMEM((depth, width), jnp.float32),
-            pltpu.VMEM((blocks, TILE, lanes), jnp.int16),
-            DMA((blocks,)),
+            pltpu.VMEM((blocks, TILE, width), f32),
+            pltpu.VMEM((peers, TILE, lanes), jnp.int16),
+            pltpu.VMEM((NX - 1,) + share, f32),
+            pltpu.VMEM(share[1:], f32),
+            pltpu.VMEM(share[1:], f32),
+            DMA((peers,)), DMA((peers,)),
+            DMA((NX - 1,)), DMA((NX - 1,)),
+            DMA, DMA, DMA,
         ],
-        compiler_params=pltpu.CompilerParams(vmem_limit_bytes=32 * 1024 * 1024),
-        name="gradient_and_update",
-    )(owners, rows, cots, weight, one, two)
-
-
-def place_kernel(slot_ref, got_ref, weight_ref, first_ref, second_ref):
-    capacity, _, width = weight_ref.shape[1:]
+        compiler_params=pltpu.CompilerParams(
+            collective_id=1, has_side_effects=True, vmem_limit_bytes=32 * 1024 * 1024
+        ),
+        name="update_and_exchange",
+    )(tile_of, rows, cots, weight, one, two, *shares)
+
+
+PER = 4
+
+
+def place_kernel(from_ref, inbox_ref, weight_ref, first_ref, second_ref, held, sems):
+    width = weight_ref.shape[3]
+    capacity = held.shape[0]
     full = width // 128 * 128
     rest = width - full
     step = pl.program_id(0)
-    some = got_ref.shape[0]
+
+    def fetch(s):
+        at = jnp.maximum(from_ref[s], 0)
+        return pltpu.make_async_copy(inbox_ref.at[at], held.at[s], sems.at[s])
 
     @pl.when(step == 0)
     def _():
-        for ref in (weight_ref, first_ref, second_ref):
-            ref[...] = jnp.zeros_like(ref)
-
-    def one(p, carry):
-        slot = slot_ref[step * some + p]
-
-        @pl.when(slot < capacity)
+        def start(s, carry):
+            fetch(s).start()
+            return carry
+
+        lax.fori_loop(0, capacity, start, 0)
+
+    for j in range(PER):
+        s = step * PER + j
+        fetch(s).wait()
+
+        @pl.when(from_ref[s] >= 0)
         def _():
-            q = got_ref[p].astype(jnp.int32)
+            q = held[s].astype(jnp.int32)
             end = q[:, 3 * full:]
             pf = jnp.exp2(end[:, 3 * rest:3 * rest + 1].astype(jnp.float32)) * (1.0 / TOP)
             ps = jnp.exp2(end[:, 3 * rest + 1:3 * rest + 2].astype(jnp.float32)) * (1.0 / TOP)
-            first_ref[0, slot, :, :full] = q[:, :full].astype(jnp.float32) * pf
-            first_ref[0, slot, :, full:] = end[:, :rest].astype(jnp.float32) * pf
-            second_ref[0, slot, :, :full] = q[:, full:2 * full].astype(jnp.float32) * ps
-            second_ref[0, slot, :, full:] = end[:, rest:2 * rest].astype(jnp.float32) * ps
-            weight_ref[0, slot, :, :full] = value_of(q[:, 2 * full:3 * full]).astype(jnp.bfloat16)
-            weight_ref[0, slot, :, full:] = value_of(end[:, 2 * rest:3 * rest]).astype(jnp.bfloat16)
-
-        return carry
-
-    lax.fori_loop(0, got_ref.shape[0], one, 0)
-
-
-def place(slots, got, capacity, width):
+            first_ref[0, j, :, :full] = q[:, :full].astype(jnp.float32) * pf
+            first_ref[0, j, :, full:] = end[:, :rest].astype(jnp.float32) * pf
+            second_ref[0, j, :, :full] = q[:, full:2 * full].astype(jnp.float32) * ps
+            second_ref[0, j, :, full:] = end[:, rest:2 * rest].astype(jnp.float32) * ps
+            weight_ref[0, j, :, :full] = value_of(q[:, 2 * full:3 * full]).astype(jnp.bfloat16)
+            weight_ref[0, j, :, full:] = value_of(end[:, 2 * rest:3 * rest]).astype(jnp.bfloat16)
+
+        @pl.when(from_ref[s] < 0)
+        def _():
+            for ref in (weight_ref, first_ref, second_ref):
+                ref[0, j] = jnp.zeros(ref.shape[2:], ref.dtype)
+
+
+def place(source, inbox, capacity, width):
     shape = (1, capacity, TILE, width)
+    block = pl.BlockSpec((1, PER, TILE, width), lambda i: (0, i, 0, 0))
     return pl.pallas_call(
         place_kernel,
         out_shape=(
@@ -434,12 +503,16 @@
             jax.ShapeDtypeStruct(shape, jnp.float32),
             jax.ShapeDtypeStruct(shape, jnp.float32),
         ),
-        grid=(8,),
-        in_specs=[SMEM, pl.BlockSpec((got.shape[0] // 8,) + got.shape[1:], lambda i: (i, 0, 0))],
-        out_specs=(pl.BlockSpec(shape, lambda i: (0, 0, 0, 0)),) * 3,
-        compiler_params=pltpu.CompilerParams(vmem_limit_bytes=40 * 1024 * 1024),
+        grid=(capacity // PER,),
+        in_specs=[SMEM, HBM],
+        out_specs=(block,) * 3,
+        scratch_shapes=[
+            pltpu.VMEM((capacity,) + inbox.shape[1:], jnp.int16),
+            DMA((capacity,)),
+        ],
+        compiler_params=pltpu.CompilerParams(vmem_limit_bytes=32 * 1024 * 1024),
         name="place_tiles",
-    )(slots, got)
+    )(source, pltpu.with_memory_space_constraint(inbox, pltpu.HBM))
 
 
 def on_device(features, weight, moment_one, moment_two, cotangent, new_owner, new_slot):
@@ -451,14 +524,18 @@
     a, b, tables, cots, weight_rows, one, two = gather(
         new_owner[0], new_slot[0], features, cotangent.T, weight.T, moment_one.T, moment_two.T
     )
-    rows, own, *shares = project(a, b, weight.T)
-    projected = sum_shares(own, shares).T
-    outbox = update(owners, rows, cots, weight_rows, one, two, peers)
+    rows, *shares = project(a, b, weight.T)
+    every = lax.broadcasted_iota(jnp.int32, (blocks, peers), 1)
+    index = lax.broadcasted_iota(jnp.int32, (blocks, peers), 0)
+    tile_of = jnp.sum(jnp.where(owners[:, None] == every, index, 0), axis=0)
+    inbox, total = exchange(tile_of, rows, cots, weight_rows, one, two, shares, peers)
     mine = tables[:, 0, :blocks] == lax.axis_index("wide")
     dest = jnp.min(jnp.where(mine, tables[:, 1, :blocks], capacity), axis=1)
-    inbox = lax.all_to_all(outbox, "wide", split_axis=0, concat_axis=0, tiled=True)
-    moved = place(dest, inbox, capacity, width)
-    return (projected,) + tuple(moved)
+    slot = lax.broadcasted_iota(jnp.int32, (peers, capacity), 1)
+    source = lax.broadcasted_iota(jnp.int32, (peers, capacity), 0)
+    source = jnp.max(jnp.where(dest[:, None] == slot, source, -1), axis=0)
+    moved = place(source, inbox, capacity, width)
+    return (total.T,) + tuple(moved)
 
 
 def solution(mesh):

time: 183 us -> 158 us (0.86)
  the two profiles are of different devices: /device:TPU:43 before, /device:TPU:1 now
where the time goes in v2:
time: 158 us; the launch traced here: 157 us
  Pallas kernels  152 us (96%)
  other arithmetic  2.19 us (1%)
  local copies, waits for them, and re-layouts  1.98 us (1%)
    pallas_call x1, Pallas kernels, exchange(): pl.pallas_call(exchange_kernel, out_shape=(pltpu.HBM((peers, TILE, lanes)...  103 us
    pallas_call x1, Pallas kernels, gather(): pl.pallas_call(gather_kernel, out_shape=(jax.ShapeDtypeStruct((NZ, NY, NC...  39.8 us
    pallas_call x1, Pallas kernels, place(): pl.pallas_call(place_kernel, out_shape=(jax.ShapeDtypeStruct(shape, jnp.b...  7.25 us

profile of v2, /device:TPU:1, one launch (start us, length us, event | category | flops | bytes accessed | tf_op | source)
XLA Modules:
  0.0 156.7 jit_solution(12193759610960254511)
XLA Ops:
  0.6 0.0 copy-start
  0.6 0.8 select_reduce_fusion.1.tile_ref
  1.4 0.0 copy-start.1
  1.4 0.6 copy-done.1
  2.1 0.0 copy-start.2
  2.1 0.7 copy-done.2
  2.8 39.8 %gather_blocks.1 = (bf16[4,8,2,16,1024]{4,3,2,1,0:T(8,128)(2,1)S(1)}, bf16[4,8,2,16,512]{4,3,2,1,0:T(8,128)(2,1)S(1)}, s32[4,8,2,8,128]{4,3,2,1,0:T(8,128)S(1)},...) custom-call(s32[1,24]{1,0:T(1,128)S(1)} %bitcast.24, ...), custom_call_target="tpu_custom_call" | custom-call | tf_op jit(solution)/shard_map/gather_blocks/pallas_call | solution.py:187
  42.6 1.3 fusion
  43.9 0.1 select_reduce_fusion.from_ref
  44.0 0.0 copy-done
  44.0 1.8 %arrange_and_project.1 = (bf16[768,2048]{1,0:T(8,128)(2,1)S(1)}, f32[2,288,256]{2,1,0:T(8,128)S(1)}, f32[2,288,256]{2,1,0:T(8,128)S(1)}, f32[2,288,256]{2,1,0:T(8,128)S(1)}, f32[2,288,256]{2,1,0:T(8,128)S(1)}) custom-call(bf16[64,16,1024]{2,1,0:T(8,128)(2,1)S(1)} %bitcast.14, bf16[64,16,512]{2,1,0:T(8,128)(2,1)S(1)} %bitcast.19, bf16[288,768]{1,0:T(8,128)(2,1)S(1)} %bitcast.16), custom_call_target="tpu_custom_call" | custom-call | tf_op jit(solution)/shard_map/arrange_and_project/pallas_call | solution.py:267
  45.8 103.0 %update_and_exchange.1 = (s16[64,32,896]{2,1,0:T(8,128)(2,1)}, bf16[288,256]{1,0:T(8,128)(2,1)S(1)}) custom-call(s32[64]{0:T(128)S(1)} %select_reduce_fusion.1.tile_ref, bf16[768,2048]{1,0:T(8,128)(2,1)S(1)} %get-tuple-element.23.f_ref, bf16[8,288,256]{2,1,0:T(8,128)(2,1)S(1)} %get-tuple-element.24.c_ref, bf16[24,32,288]{2,1,0:T(8,128)(2,1)S(1)} %bitcast.20, ...), custom_call_target="tpu_custom_call" | custom-call | tf_op jit(solution)/shard_map/update_and_exchange/pallas_call | solution.py:426
  148.8 7.2 %place_tiles.1 = (bf16[1,28,32,288]{3,2,1,0:T(8,128)(2,1)}, f32[1,28,32,288]{3,2,1,0:T(8,128)}, f32[1,28,32,288]{3,2,1,0:T(8,128)}) custom-call(s32[28]{0:T(128)S(1)} %select_reduce_fusion.from_ref, s16[64,32,896]{2,1,0:T(8,128)(2,1)} %get-tuple-element.34.inbox_ref), custom_call_target="tpu_custom_call" | custom-call | tf_op jit(solution)/shard_map/place_tiles/pallas_call | solution.py:499
  156.1 0.7 copy.12
Async XLA Ops:
  0.6 43.4 %copy-start = (bf16[768,288]{0,1:T(8,128)(2,1)S(1)}, bf16[768,288]{0,1:T(8,128)(2,1)}, u32[]{:S(2)}) copy-start(bf16[768,288]{0,1:T(8,128)(2,1)} %param.8) | copy-start | bytes 1327108
  1.4 0.7 copy-start.1
  2.1 0.7 copy-start.2

commit v3 on v2

--- a/solution.py
+++ b/solution.py
@@ -35,13 +35,14 @@
 
 
 HEAD = 1024
+AHEAD = 9
 KEEP = 1536
 
 
 def gather_kernel(
-    owner_ref, slot_ref, x_in, c_in, wt_in, onet_in, twot_in,
-    a_ref, b_ref, t_ref, call_ref, w_ref, one_ref, two_ref,
-    x_ref, wt_ref, onet_ref, twot_ref,
+    owner_in, slot_in, x_in, c_in, wt_in, onet_in, twot_in,
+    a_ref, b_ref, t_ref, tile_ref, call_ref, w_ref, one_ref, two_ref,
+    owner_ref, slot_ref, x_ref, wt_ref, onet_ref, twot_ref,
     zs, zr, rs, rr, ls, lr, ss, sr, bs, br, bzs, bzr, bss, bsr,
     ts, tr, tzs, tzr, tss, tsr, ns, nr, loc,
 ):
@@ -68,12 +69,11 @@
         for i, (src, dst) in enumerate((
             (x_in, x_ref), (c_in, call_ref.at[n]),
             (onet_in, onet_ref), (twot_in, twot_ref), (wt_in, wt_ref),
+            (owner_in, owner_ref), (slot_in, slot_ref),
         ))
     ]
     for copy in own:
         copy.start()
-    t_ref[z, y, c, 0:1, :owner_ref.shape[1]] = owner_ref[...]
-    t_ref[z, y, c, 1:2, :slot_ref.shape[1]] = slot_ref[...]
     own[0].wait()
 
     rows = x_ref.shape[0]
@@ -83,6 +83,10 @@
     for k in range(HEAD // extra):
         a_ref[z, y, c, rows:, k * extra:(k + 1) * extra] = x_ref[4 * k:4 * k + 4, KEEP:]
     b_ref[z, y, c, rows:, :] = x_ref[rows - 4:, KEEP:]
+    own[5].wait()
+    own[6].wait()
+    t_ref[z, y, c, 0:1, :owner_ref.shape[1]] = owner_ref[...]
+    t_ref[z, y, c, 1:2, :slot_ref.shape[1]] = slot_ref[...]
     own[1].wait()
 
     pl.semaphore_wait(barrier, len(peers))
@@ -95,11 +99,11 @@
         copy.start()
         return copy
 
+    b_copies = [
+        send(b_ref.at[z, y, c], bs.at[k], br.at[k], y_peers[k]) for k in range(NY - 1)
+    ]
     z_copies = [
         send(a_ref.at[z, y, c], zs.at[k], zr.at[k], z_peers[k]) for k in range(NZ - 1)
-    ]
-    b_copies = [
-        send(b_ref.at[z, y, c], bs.at[k], br.at[k], y_peers[k]) for k in range(NY - 1)
     ]
     across = send(call_ref.at[n], ns.at[0], nr.at[0], partner)
     x_copies = [
@@ -131,18 +135,25 @@
                     from_left[s, k] = send(block(k, y - s), rs.at[s, k], rr.at[s, k], right)
                 if not last or i % 2 == 1:
                     from_right[s, k] = send(block(k, y + s), ls.at[s, k], lr.at[s, k], left)
+            if s == 0 and k == 0:
+                for copy in b_copies:
+                    copy.wait_recv()
+                bz = [
+                    send(b_ref.at[z, :, c], bzs.at[j], bzr.at[j], z_peers[j])
+                    for j in range(NZ - 1)
+                ]
         to_sib.append(send(a_ref.at[:, lax.rem(y - s + NY, NY), c], ss.at[2 * s], sr.at[2 * s], sibling))
         if 0 < s < half:
             to_sib.append(
                 send(a_ref.at[:, lax.rem(y + s, NY), c], ss.at[2 * s - 1], sr.at[2 * s - 1], sibling)
             )
         if s == 0:
-            for copy in b_copies:
-                copy.wait_recv()
-            bz = [
-                send(b_ref.at[z, :, c], bzs.at[k], bzr.at[k], z_peers[k]) for k in range(NZ - 1)
-            ]
             sib_b = [send(b_ref.at[z, :, c], bss.at[0], bsr.at[0], sibling)]
+            lane = lax.broadcasted_iota(jnp.int32, tile_ref.shape, 1)
+            tile = jnp.zeros(tile_ref.shape, jnp.int32)
+            for t in range(owner_ref.shape[1]):
+                tile = jnp.where(lane == owner_ref[0:1, t:t + 1], t, tile)
+            tile_ref[...] = tile
             own[2].wait()
             one_ref[...] = onet_ref[...].T
         if s == 1:
@@ -184,20 +195,23 @@
     half = NY // 2
     pad = rows + rows // 3
     f32, bf16 = jnp.float32, jnp.bfloat16
-    a, b, t, call, w, one, two = pl.pallas_call(
+    a, b, t, tile, call, w, one, two = pl.pallas_call(
         gather_kernel,
         out_shape=(
             jax.ShapeDtypeStruct((NZ, NY, NC, pad, HEAD), bf16),
             jax.ShapeDtypeStruct((NZ, NY, NC, pad, KEEP - HEAD), bf16),
             jax.ShapeDtypeStruct((NZ, NY, NC, 8, 128), jnp.int32),
+            jax.ShapeDtypeStruct((1, 128), jnp.int32),
             jax.ShapeDtypeStruct((NN, cw, ct), bf16),
             jax.ShapeDtypeStruct((depth, width), bf16),
             jax.ShapeDtypeStruct((depth, width), f32),
             jax.ShapeDtypeStruct((depth, width), f32),
         ),
-        in_specs=[VMEM] * 2 + [ANY] * 5,
-        out_specs=(VMEM,) * 7,
+        in_specs=[HBM] * 7,
+        out_specs=(VMEM,) * 8,
         scratch_shapes=[
+            pltpu.VMEM(owners.shape, jnp.int32),
+            pltpu.VMEM(slots.shape, jnp.int32),
             pltpu.VMEM((rows, tokens), bf16),
             pltpu.VMEM((width, depth), bf16),
             pltpu.VMEM((width, depth), f32),
@@ -213,30 +227,27 @@
             DMA((NZ - 1,)), DMA((NZ - 1,)),
             DMA((NZ,)), DMA((NZ,)),
             DMA((NN - 1,)), DMA((NN - 1,)),
-            DMA((5,)),
+            DMA((7,)),
         ],
         compiler_params=pltpu.CompilerParams(
             collective_id=0, has_side_effects=True, vmem_limit_bytes=32 * 1024 * 1024
         ),
         name="gather_blocks",
-    )(
-        owners, slots,
-        *(pltpu.with_memory_space_constraint(v, pltpu.HBM) for v in (features, cotangent, wt, onet, twot)),
-    )
+    )(*(
+        pltpu.with_memory_space_constraint(v, pltpu.HBM)
+        for v in (owners, slots, features, cotangent, wt, onet, twot)
+    ))
     many = NZ * NY * NC
     a, b, t = (v.reshape((many,) + v.shape[3:]) for v in (a, b, t))
-    return a, b, t, call, w, one, two
-
-
-def project_kernel(a_ref, b_ref, wt_ref, f_ref, own_ref, p1_ref, p2_ref, p3_ref):
-    n = lax.axis_index("node")
-    x, high = lax.rem(n, NX), n // NX
+    return a, b, t, tile, call, w, one, two
+
+
+def arrange(a_ref, b_ref, f_ref):
     blocks, pad, _ = a_ref.shape
     rows = pad * 3 // 4
-    tokens = f_ref.shape[1] // NN
     extra = f_ref.shape[1] - KEEP
 
-    def arrange(i, carry):
+    def four(i, carry):
         at = pl.ds(pl.multiple_of(i * 4 * rows, 16), 4 * rows)
         a = a_ref[pl.ds(4 * i, 4)]
         b = b_ref[pl.ds(4 * i, 4)]
@@ -250,28 +261,7 @@
         f_ref[at, KEEP:] = jnp.concatenate(ends, axis=0)
         return carry
 
-    lax.fori_loop(0, blocks // 4, arrange, 0)
-
-    for k, out in ((1, p1_ref), (2, p2_ref), (3, p3_ref), (0, own_ref)):
-        for h in range(2):
-            node = lax.rem(high + h, 2) * NX + lax.rem(x + k, NX)
-            at = pl.ds(pl.multiple_of(node * tokens, tokens), tokens)
-            out[h] = jnp.dot(wt_ref[...], f_ref[:, at], preferred_element_type=jnp.float32)
-
-
-def project(a, b, wt):
-    blocks, pad, _ = a.shape
-    width, depth = wt.shape
-    tokens = KEEP + (KEEP // 3)
-    share = jax.ShapeDtypeStruct((2, width, tokens // NN), jnp.float32)
-    return pl.pallas_call(
-        project_kernel,
-        out_shape=(jax.ShapeDtypeStruct((depth, tokens), jnp.bfloat16),) + (share,) * NX,
-        in_specs=[VMEM] * 3,
-        out_specs=(VMEM,) * (NX + 1),
-        compiler_params=pltpu.CompilerParams(vmem_limit_bytes=32 * 1024 * 1024),
-        name="arrange_and_project",
-    )(a, b, wt)
+    lax.fori_loop(0, blocks // 4, four, 0)
 
 
 def fixed_point(x):
@@ -301,8 +291,8 @@
 
 
 def exchange_kernel(
-    tile_ref, f_ref, c_ref, w_ref, one_ref, two_ref, own_ref, p1_ref, p2_ref, p3_ref,
-    inbox_ref, out_ref, grad, outbox, got, total, across_got,
+    tile_ref, a_ref, b_ref, t_ref, c_ref, wt_ref, w_ref, one_ref, two_ref,
+    inbox_ref, out_ref, from_ref, f_ref, grad, outbox, share, got, total, across_got,
     send_sem, recv_sem, xs, xr, acs, acr, loc,
 ):
     n = lax.axis_index("node")
@@ -313,9 +303,16 @@
     full = width // 128 * 128
     rest = width - full
 
+    z, y, c = place_of(w)
+    x, high = lax.rem(n, NX), n // NX
+
     def peer_of(i):
         step = lax.rem(i * 27, many)
-        return lax.rem(w + step, many), step
+        sign = 1 - 2 * c
+        dz, dy, dc = place_of(step)
+        to_z = lax.rem(z + NZ + sign * dz, NZ)
+        to_y = lax.rem(y + NY + sign * dy, NY)
+        return (to_z * NY + to_y) * NC + lax.rem(c + dc, NC), step
 
     barrier = pltpu.get_barrier_semaphore()
     for peer in [partner] + x_peers:
@@ -328,6 +325,7 @@
 
     lax.fori_loop(1, many, greet, 0)
 
+    arrange(a_ref, b_ref, f_ref)
     part = grad.shape[0] // 3
     tokens = c_ref.shape[2]
 
@@ -346,18 +344,8 @@
     lax.fori_loop(0, 3, multiply, 0)
     pl.semaphore_wait(barrier, many - 1 + NX)
 
-    shares = (p1_ref, p2_ref, p3_ref)
-    x_copies = []
-    for k in range(NX - 1):
-        copy = pltpu.make_async_remote_copy(
-            src_ref=shares[k], dst_ref=got.at[k], send_sem=xs.at[k], recv_sem=xr.at[k],
-            device_id=x_peers[k], device_id_type=MESH,
-        )
-        copy.start()
-        x_copies.append(copy)
-
     def pack(p):
-        b = tile_ref[p]
+        b = tile_ref[0, p]
         g = grad[b]
         first = 0.9 * one_ref[b] + 0.1 * g
         second = 0.999 * two_ref[b] + 0.001 * g * g
@@ -387,20 +375,47 @@
         copy_to(p, step).start()
         return carry
 
-    lax.fori_loop(1, many, send, 0)
+    lax.fori_loop(1, AHEAD, send, 0)
+
+    def partial(k, half):
+        node = lax.rem(high + half, 2) * NX + lax.rem(x + k, NX)
+        at = pl.ds(pl.multiple_of(node * tokens, tokens), tokens)
+        share[k, half] = jnp.dot(wt_ref[...], f_ref[:, at], preferred_element_type=jnp.float32)
+
+    x_copies = []
+    for k in range(1, NX):
+        for half in range(2):
+            partial(k, half)
+        copy = pltpu.make_async_remote_copy(
+            src_ref=share.at[k], dst_ref=got.at[k - 1],
+            send_sem=xs.at[k - 1], recv_sem=xr.at[k - 1],
+            device_id=x_peers[k - 1], device_id_type=MESH,
+        )
+        copy.start()
+        x_copies.append(copy)
+    lax.fori_loop(AHEAD, many, send, 0)
+    for half in range(2):
+        partial(0, half)
     pack(w)
     mine = pltpu.make_async_copy(outbox.at[w], inbox_ref.at[w], loc)
     mine.start()
 
+    blocks = grad.shape[0]
+    lane = lax.broadcasted_iota(jnp.int32, (many, 128), 1)
+    ours = jnp.logical_and(t_ref[:, 0, :] == w, lane < blocks)
+    slot = jnp.min(jnp.where(ours, t_ref[:, 1, :], 128), axis=1, keepdims=True)
+    source = lax.broadcasted_iota(jnp.int32, (many, 128), 0)
+    from_ref[...] = jnp.max(jnp.where(slot == lane, source, -1), axis=0, keepdims=True)
+
     for copy in x_copies:
         copy.wait_recv()
-    total[...] = own_ref[1] + got[0, 1] + got[1, 1] + got[2, 1]
+    total[...] = share[0, 1] + got[0, 1] + got[1, 1] + got[2, 1]
     across = pltpu.make_async_remote_copy(
         src_ref=total, dst_ref=across_got, send_sem=acs, recv_sem=acr,
         device_id=partner, device_id_type=MESH,
     )
     across.start()
-    near = own_ref[0] + got[0, 0] + got[1, 0] + got[2, 0]
+    near = share[0, 0] + got[0, 0] + got[1, 0] + got[2, 0]
     across.wait_recv()
     out_ref[...] = (near + across_got[...]).astype(jnp.bfloat16)
 
@@ -416,27 +431,31 @@
         copy.wait_send()
 
 
-def exchange(tile_of, rows, cots, weight, one, two, shares, peers):
+def exchange(tile_of, a, b, tables, cots, wt, weight, one, two):
     depth, width = weight.shape
     lanes = 3 * (width // 128 * 128) + 128
     blocks = depth // TILE
-    share = shares[0].shape
+    peers = tables.shape[0]
+    tokens = cots.shape[2]
     f32 = jnp.float32
     weight, one, two = (v.reshape(blocks, TILE, width) for v in (weight, one, two))
     return pl.pallas_call(
         exchange_kernel,
         out_shape=(
             pltpu.HBM((peers, TILE, lanes), jnp.int16),
-            jax.ShapeDtypeStruct(share[1:], jnp.bfloat16),
+            jax.ShapeDtypeStruct((width, tokens), jnp.bfloat16),
+            jax.ShapeDtypeStruct((1, 128), jnp.int32),
         ),
-        in_specs=[SMEM] + [VMEM] * 9,
-        out_specs=(HBM, VMEM),
+        in_specs=[SMEM] + [VMEM] * 8,
+        out_specs=(HBM, VMEM, VMEM),
         scratch_shapes=[
+            pltpu.VMEM((depth, tokens * NN), jnp.bfloat16),
             pltpu.VMEM((blocks, TILE, width), f32),
             pltpu.VMEM((peers, TILE, lanes), jnp.int16),
-            pltpu.VMEM((NX - 1,) + share, f32),
-            pltpu.VMEM(share[1:], f32),
-            pltpu.VMEM(share[1:], f32),
+            pltpu.VMEM((NX, 2, width, tokens), f32),
+            pltpu.VMEM((NX - 1, 2, width, tokens), f32),
+            pltpu.VMEM((width, tokens), f32),
+            pltpu.VMEM((width, tokens), f32),
             DMA((peers,)), DMA((peers,)),
             DMA((NX - 1,)), DMA((NX - 1,)),
             DMA, DMA, DMA,
@@ -445,13 +464,15 @@
             collective_id=1, has_side_effects=True, vmem_limit_bytes=32 * 1024 * 1024
         ),
         name="update_and_exchange",
-    )(tile_of, rows, cots, weight, one, two, *shares)
-
-
-PER = 4
-
-
-def place_kernel(from_ref, inbox_ref, weight_ref, first_ref, second_ref, held, sems):
+    )(tile_of, a, b, tables, cots, wt, weight, one, two)
+
+
+PER = 7
+
+
+def place_kernel(
+    from_ref, inbox_ref, total_ref, weight_ref, first_ref, second_ref, out_ref, held, sems
+):
     width = weight_ref.shape[3]
     capacity = held.shape[0]
     full = width // 128 * 128
@@ -459,7 +480,7 @@
     step = pl.program_id(0)
 
     def fetch(s):
-        at = jnp.maximum(from_ref[s], 0)
+        at = jnp.maximum(from_ref[0, s], 0)
         return pltpu.make_async_copy(inbox_ref.at[at], held.at[s], sems.at[s])
 
     @pl.when(step == 0)
@@ -469,73 +490,58 @@
             return carry
 
         lax.fori_loop(0, capacity, start, 0)
+        out_ref[...] = total_ref[...]
 
     for j in range(PER):
         s = step * PER + j
         fetch(s).wait()
-
-        @pl.when(from_ref[s] >= 0)
-        def _():
-            q = held[s].astype(jnp.int32)
-            end = q[:, 3 * full:]
-            pf = jnp.exp2(end[:, 3 * rest:3 * rest + 1].astype(jnp.float32)) * (1.0 / TOP)
-            ps = jnp.exp2(end[:, 3 * rest + 1:3 * rest + 2].astype(jnp.float32)) * (1.0 / TOP)
-            first_ref[0, j, :, :full] = q[:, :full].astype(jnp.float32) * pf
-            first_ref[0, j, :, full:] = end[:, :rest].astype(jnp.float32) * pf
-            second_ref[0, j, :, :full] = q[:, full:2 * full].astype(jnp.float32) * ps
-            second_ref[0, j, :, full:] = end[:, rest:2 * rest].astype(jnp.float32) * ps
-            weight_ref[0, j, :, :full] = value_of(q[:, 2 * full:3 * full]).astype(jnp.bfloat16)
-            weight_ref[0, j, :, full:] = value_of(end[:, 2 * rest:3 * rest]).astype(jnp.bfloat16)
-
-        @pl.when(from_ref[s] < 0)
-        def _():
-            for ref in (weight_ref, first_ref, second_ref):
-                ref[0, j] = jnp.zeros(ref.shape[2:], ref.dtype)
-
-
-def place(source, inbox, capacity, width):
-    shape = (1, capacity, TILE, width)
-    block = pl.BlockSpec((1, PER, TILE, width), lambda i: (0, i, 0, 0))
+        some = from_ref[0, s] >= 0
+        q = jnp.where(some, held[s].astype(jnp.int32), 0)
+        end = q[:, 3 * full:]
+        pf = jnp.exp2(end[:, 3 * rest:3 * rest + 1].astype(jnp.float32)) * (1.0 / TOP)
+        ps = jnp.exp2(end[:, 3 * rest + 1:3 * rest + 2].astype(jnp.float32)) * (1.0 / TOP)
+        first_ref[0, j, :, :full] = q[:, :full].astype(jnp.float32) * pf
+        first_ref[0, j, :, full:] = end[:, :rest].astype(jnp.float32) * pf
+        second_ref[0, j, :, :full] = q[:, full:2 * full].astype(jnp.float32) * ps
+        second_ref[0, j, :, full:] = end[:, rest:2 * rest].astype(jnp.float32) * ps
+        weight_ref[0, j, :, :full] = value_of(q[:, 2 * full:3 * full]).astype(jnp.bfloat16)
+        weight_ref[0, j, :, full:] = value_of(end[:, 2 * rest:3 * rest]).astype(jnp.bfloat16)
+
+
+def place(source, inbox, total, capacity):
+    shape = (1, capacity, TILE, total.shape[0])
+    block = pl.BlockSpec((1, PER) + shape[2:], lambda i: (0, i, 0, 0))
+    whole = pl.BlockSpec(total.shape, lambda i: (0, 0))
     return pl.pallas_call(
         place_kernel,
         out_shape=(
             jax.ShapeDtypeStruct(shape, jnp.bfloat16),
             jax.ShapeDtypeStruct(shape, jnp.float32),
             jax.ShapeDtypeStruct(shape, jnp.float32),
+            jax.ShapeDtypeStruct(total.shape, total.dtype),
         ),
         grid=(capacity // PER,),
-        in_specs=[SMEM, HBM],
-        out_specs=(block,) * 3,
+        in_specs=[SMEM, HBM, whole],
+        out_specs=(block,) * 3 + (whole,),
         scratch_shapes=[
             pltpu.VMEM((capacity,) + inbox.shape[1:], jnp.int16),
             DMA((capacity,)),
         ],
         compiler_params=pltpu.CompilerParams(vmem_limit_bytes=32 * 1024 * 1024),
         name="place_tiles",
-    )(source, pltpu.with_memory_space_constraint(inbox, pltpu.HBM))
+    )(source, pltpu.with_memory_space_constraint(inbox, pltpu.HBM), total)
 
 
 def on_device(features, weight, moment_one, moment_two, cotangent, new_owner, new_slot):
-    peers = lax.axis_size("wide")
-    owners = new_owner.reshape(-1)
-    blocks = owners.shape[0]
+    blocks = new_owner.shape[2]
     capacity = blocks + blocks // 6
-    width = weight.shape[1]
-    a, b, tables, cots, weight_rows, one, two = gather(
-        new_owner[0], new_slot[0], features, cotangent.T, weight.T, moment_one.T, moment_two.T
+    wt = weight.T
+    a, b, tables, tile_of, cots, weight_rows, one, two = gather(
+        new_owner[0], new_slot[0], features, cotangent.T, wt, moment_one.T, moment_two.T
     )
-    rows, *shares = project(a, b, weight.T)
-    every = lax.broadcasted_iota(jnp.int32, (blocks, peers), 1)
-    index = lax.broadcasted_iota(jnp.int32, (blocks, peers), 0)
-    tile_of = jnp.sum(jnp.where(owners[:, None] == every, index, 0), axis=0)
-    inbox, total = exchange(tile_of, rows, cots, weight_rows, one, two, shares, peers)
-    mine = tables[:, 0, :blocks] == lax.axis_index("wide")
-    dest = jnp.min(jnp.where(mine, tables[:, 1, :blocks], capacity), axis=1)
-    slot = lax.broadcasted_iota(jnp.int32, (peers, capacity), 1)
-    source = lax.broadcasted_iota(jnp.int32, (peers, capacity), 0)
-    source = jnp.max(jnp.where(dest[:, None] == slot, source, -1), axis=0)
-    moved = place(source, inbox, capacity, width)
-    return (total.T,) + tuple(moved)
+    inbox, total, source = exchange(tile_of, a, b, tables, cots, wt, weight_rows, one, two)
+    *moved, projected = place(source, inbox, total, capacity)
+    return (projected.T,) + tuple(moved)
 
 
 def solution(mesh):

time: 158 us -> 152 us (0.962)
  other arithmetic: 2.19 us -> 0 us
  local copies, waits for them, and re-layouts: 1.98 us -> 0.01 us
    unnamed x7 -> x2, local copies, waits for them, and re-layouts: 1.98 us -> 0.01 us
    pallas_call x1 -> x0, Pallas kernels: 1.78 us -> none  [project(): pl.pallas_call(project_kernel, out_shape=(jax.ShapeDtypeStruct((depth, to...]
where the time goes in v3:
time: 152 us; the launch traced here: 151 us
  Pallas kernels  151 us (99%)
    pallas_call x1, Pallas kernels, exchange(): pl.pallas_call(exchange_kernel, out_shape=(pltpu.HBM((peers, TILE, lanes)...  103 us
    pallas_call x1, Pallas kernels, gather(): pl.pallas_call(gather_kernel, out_shape=(jax.ShapeDtypeStruct((NZ, NY, NC...  40.1 us
    pallas_call x1, Pallas kernels, place(): pl.pallas_call(place_kernel, out_shape=(jax.ShapeDtypeStruct(shape, jnp.b...  7.27 us

profile of v3, /device:TPU:1, one launch (start us, length us, event | category | flops | bytes accessed | tf_op | source)
XLA Modules:
  0.0 151.4 jit_solution(3652859502166550656)
XLA Ops:
  0.6 0.0 copy-start
  0.6 40.1 %gather_blocks.1 = (bf16[4,8,2,16,1024]{4,3,2,1,0:T(8,128)(2,1)S(1)}, bf16[4,8,2,16,512]{4,3,2,1,0:T(8,128)(2,1)S(1)}, s32[4,8,2,8,128]{4,3,2,1,0:T(8,128)S(1)},...) custom-call(s32[1,24]{1,0:T(1,128)} %bitcast.24, ...), custom_call_target="tpu_custom_call" | custom-call | tf_op jit(solution)/shard_map/gather_blocks/pallas_call | solution.py:198
  40.7 0.0 copy-done
  40.7 103.4 %update_and_exchange.1 = (s16[64,32,896]{2,1,0:T(8,128)(2,1)}, bf16[288,256]{1,0:T(8,128)(2,1)S(1)}, s32[1,128]{1,0:T(1,128)S(1)}) custom-call(s32[1,128]{1,0:T(1,128)S(1)} %get-tuple-element.19.tile_ref, bf16[64,16,1024]{2,1,0:T(8,128)(2,1)S(1)} %bitcast.13, bf16[64,16,512]{2,1,0:T(8,128)(2,1)S(1)} %bitcast.18, s32[64,8,128]{2,1,0:T(8,128)S(1)} %bitcast.20, ...), custom_call_target="tpu_custom_call" | custom-call | tf_op jit(solution)/shard_map/update_and_exchange/pallas_call | solution.py:442
  144.1 7.3 %place_tiles.1 = (bf16[1,28,32,288]{3,2,1,0:T(8,128)(2,1)}, f32[1,28,32,288]{3,2,1,0:T(8,128)}, f32[1,28,32,288]{3,2,1,0:T(8,128)}, bf16[288,256]{1,0:T(8,128)(2,1)}) custom-call(s32[1,128]{1,0:T(1,128)S(1)} %get-tuple-element.27.from_ref, s16[64,32,896]{2,1,0:T(8,128)(2,1)} %get-tuple-element.28.inbox_ref, bf16[288,256]{1,0:T(8,128)(2,1)S(1)} %get-tuple-element.29.total_ref), custom_call_target="tpu_custom_call" | custom-call | tf_op jit(solution)/shard_map/place_tiles/pallas_call | solution.py:515
Async XLA Ops:
  0.6 40.1 %copy-start = (bf16[768,288]{0,1:T(8,128)(2,1)S(1)}, bf16[768,288]{0,1:T(8,128)(2,1)}, u32[]{:S(2)}) copy-start(bf16[768,288]{0,1:T(8,128)(2,1)} %param.8) | copy-start | bytes 1327108

commit v4 on v3

--- a/solution.py
+++ b/solution.py
@@ -34,7 +34,7 @@
     return (lax.rem(n + NX, NN), w), [(base + lax.rem(x + k, NX), w) for k in range(1, NX)]
 
 
-HEAD = 1024
+HEAD = 1280
 AHEAD = 9
 KEEP = 1536
 
@@ -77,12 +77,14 @@
     own[0].wait()
 
     rows = x_ref.shape[0]
-    extra = (x_ref.shape[1] - KEEP)
+    extra = x_ref.shape[1] - KEEP
+    third = HEAD - 2 * extra
     a_ref[z, y, c, :rows, :] = x_ref[:, :HEAD]
     b_ref[z, y, c, :rows, :] = x_ref[:, HEAD:KEEP]
-    for k in range(HEAD // extra):
+    for k in range(2):
         a_ref[z, y, c, rows:, k * extra:(k + 1) * extra] = x_ref[4 * k:4 * k + 4, KEEP:]
-    b_ref[z, y, c, rows:, :] = x_ref[rows - 4:, KEEP:]
+    a_ref[z, y, c, rows:, 2 * extra:] = x_ref[rows - 4:, KEEP:KEEP + third]
+    b_ref[z, y, c, rows:, :] = x_ref[rows - 4:, KEEP + third:]
     own[5].wait()
     own[6].wait()
     t_ref[z, y, c, 0:1, :owner_ref.shape[1]] = owner_ref[...]
@@ -255,9 +257,9 @@
         f_ref[at, HEAD:KEEP] = jnp.concatenate([b[j, :rows] for j in range(4)], axis=0)
         ends = []
         for j in range(4):
-            for k in range(HEAD // extra):
+            for k in range(2):
                 ends.append(a[j, rows:, k * extra:(k + 1) * extra])
-            ends.append(b[j, rows:])
+            ends.append(jnp.concatenate([a[j, rows:, 2 * extra:], b[j, rows:]], axis=1))
         f_ref[at, KEEP:] = jnp.concatenate(ends, axis=0)
         return carry
 
@@ -442,12 +444,12 @@
     return pl.pallas_call(
         exchange_kernel,
         out_shape=(
-            pltpu.HBM((peers, TILE, lanes), jnp.int16),
+            jax.ShapeDtypeStruct((peers, TILE, lanes), jnp.int16),
             jax.ShapeDtypeStruct((width, tokens), jnp.bfloat16),
             jax.ShapeDtypeStruct((1, 128), jnp.int32),
         ),
         in_specs=[SMEM] + [VMEM] * 8,
-        out_specs=(HBM, VMEM, VMEM),
+        out_specs=(VMEM, VMEM, VMEM),
         scratch_shapes=[
             pltpu.VMEM((depth, tokens * NN), jnp.bfloat16),
             pltpu.VMEM((blocks, TILE, width), f32),
@@ -467,69 +469,80 @@
     )(tile_of, a, b, tables, cots, wt, weight, one, two)
 
 
-PER = 7
+PER = 4
 
 
 def place_kernel(
-    from_ref, inbox_ref, total_ref, weight_ref, first_ref, second_ref, out_ref, held, sems
+    from_ref, inbox_ref, total_ref, weight_out, first_out, second_out, out_ref,
+    weight_ref, first_ref, second_ref, sems, last,
 ):
-    width = weight_ref.shape[3]
-    capacity = held.shape[0]
+    capacity, _, width = weight_ref.shape
     full = width // 128 * 128
     rest = width - full
-    step = pl.program_id(0)
-
-    def fetch(s):
-        at = jnp.maximum(from_ref[0, s], 0)
-        return pltpu.make_async_copy(inbox_ref.at[at], held.at[s], sems.at[s])
-
-    @pl.when(step == 0)
-    def _():
-        def start(s, carry):
-            fetch(s).start()
-            return carry
-
-        lax.fori_loop(0, capacity, start, 0)
-        out_ref[...] = total_ref[...]
-
-    for j in range(PER):
-        s = step * PER + j
-        fetch(s).wait()
-        some = from_ref[0, s] >= 0
-        q = jnp.where(some, held[s].astype(jnp.int32), 0)
-        end = q[:, 3 * full:]
-        pf = jnp.exp2(end[:, 3 * rest:3 * rest + 1].astype(jnp.float32)) * (1.0 / TOP)
-        ps = jnp.exp2(end[:, 3 * rest + 1:3 * rest + 2].astype(jnp.float32)) * (1.0 / TOP)
-        first_ref[0, j, :, :full] = q[:, :full].astype(jnp.float32) * pf
-        first_ref[0, j, :, full:] = end[:, :rest].astype(jnp.float32) * pf
-        second_ref[0, j, :, :full] = q[:, full:2 * full].astype(jnp.float32) * ps
-        second_ref[0, j, :, full:] = end[:, rest:2 * rest].astype(jnp.float32) * ps
-        weight_ref[0, j, :, :full] = value_of(q[:, 2 * full:3 * full]).astype(jnp.bfloat16)
-        weight_ref[0, j, :, full:] = value_of(end[:, 2 * rest:3 * rest]).astype(jnp.bfloat16)
+    whole = pltpu.make_async_copy(total_ref, out_ref, last)
+    whole.start()
+
+    def writes(i):
+        at = pl.ds(i * PER, PER)
+        return [
+            pltpu.make_async_copy(ref.at[at], out.at[0, at], sems.at[k, i])
+            for k, (ref, out) in enumerate((
+                (first_ref, first_out), (second_ref, second_out), (weight_ref, weight_out),
+            ))
+        ]
+
+    def some(i, carry):
+        for j in range(PER):
+            s = i * PER + j
+            p = from_ref[0, s]
+            q = jnp.where(p >= 0, inbox_ref[jnp.maximum(p, 0)].astype(jnp.int32), 0)
+            end = q[:, 3 * full:]
+            pf = jnp.exp2(end[:, 3 * rest:3 * rest + 1].astype(jnp.float32)) * (1.0 / TOP)
+            ps = jnp.exp2(end[:, 3 * rest + 1:3 * rest + 2].astype(jnp.float32)) * (1.0 / TOP)
+            first_ref[s, :, :full] = q[:, :full].astype(jnp.float32) * pf
+            first_ref[s, :, full:] = end[:, :rest].astype(jnp.float32) * pf
+            second_ref[s, :, :full] = q[:, full:2 * full].astype(jnp.float32) * ps
+            second_ref[s, :, full:] = end[:, rest:2 * rest].astype(jnp.float32) * ps
+            weight_ref[s, :, :full] = value_of(q[:, 2 * full:3 * full]).astype(jnp.bfloat16)
+            weight_ref[s, :, full:] = value_of(end[:, 2 * rest:3 * rest]).astype(jnp.bfloat16)
+        for copy in writes(i):
+            copy.start()
+        return carry
+
+    lax.fori_loop(0, capacity // PER, some, 0)
+
+    def finish(i, carry):
+        for copy in writes(i):
+            copy.wait()
+        return carry
+
+    lax.fori_loop(0, capacity // PER, finish, 0)
+    whole.wait()
 
 
 def place(source, inbox, total, capacity):
     shape = (1, capacity, TILE, total.shape[0])
-    block = pl.BlockSpec((1, PER) + shape[2:], lambda i: (0, i, 0, 0))
-    whole = pl.BlockSpec(total.shape, lambda i: (0, 0))
+    bf16, f32 = jnp.bfloat16, jnp.float32
     return pl.pallas_call(
         place_kernel,
         out_shape=(
-            jax.ShapeDtypeStruct(shape, jnp.bfloat16),
-            jax.ShapeDtypeStruct(shape, jnp.float32),
-            jax.ShapeDtypeStruct(shape, jnp.float32),
-            jax.ShapeDtypeStruct(total.shape, total.dtype),
+            pltpu.HBM(shape, bf16),
+            pltpu.HBM(shape, f32),
+            pltpu.HBM(shape, f32),
+            pltpu.HBM(total.shape, total.dtype),
         ),
-        grid=(capacity // PER,),
-        in_specs=[SMEM, HBM, whole],
-        out_specs=(block,) * 3 + (whole,),
+        in_specs=[SMEM, VMEM, VMEM],
+        out_specs=(HBM,) * 4,
         scratch_shapes=[
-            pltpu.VMEM((capacity,) + inbox.shape[1:], jnp.int16),
-            DMA((capacity,)),
+            pltpu.VMEM(shape[1:], bf16),
+            pltpu.VMEM(shape[1:], f32),
+            pltpu.VMEM(shape[1:], f32),
+            DMA((3, capacity // PER)),
+            DMA,
         ],
         compiler_params=pltpu.CompilerParams(vmem_limit_bytes=32 * 1024 * 1024),
         name="place_tiles",
-    )(source, pltpu.with_memory_space_constraint(inbox, pltpu.HBM), total)
+    )(source, inbox, total)
 
 
 def on_device(features, weight, moment_one, moment_two, cotangent, new_owner, new_slot):

time: 152 us -> 147 us (0.967)
  Pallas kernels: 151 us -> 145 us
    pallas_call x2, Pallas kernels: 111 us -> 106 us  [the longest x1 103 us: exchange(): pl.pallas_call(exchange_kernel, out_shape=(jax.ShapeDtypeStruct((peers, T...]
where the time goes in v4:
time: 147 us; the launch traced here: 146 us
  Pallas kernels  145 us (99%)
    pallas_call x1, Pallas kernels, exchange(): pl.pallas_call(exchange_kernel, out_shape=(jax.ShapeDtypeStruct((peers, T...  103 us
    pallas_call x1, Pallas kernels, gather(): pl.pallas_call(gather_kernel, out_shape=(jax.ShapeDtypeStruct((NZ, NY, NC...  39.2 us
    pallas_call x1, Pallas kernels, place(): pl.pallas_call(place_kernel, out_shape=(pltpu.HBM(shape, bf16), pltpu.HBM...  3.22 us

profile of v4, /device:TPU:1, one launch (start us, length us, event | category | flops | bytes accessed | tf_op | source)
XLA Modules:
  0.0 146.1 jit_solution(4420781156460628302)
XLA Ops:
  0.6 0.0 copy-start
  0.6 39.2 %gather_blocks.1 = (bf16[4,8,2,16,1280]{4,3,2,1,0:T(8,128)(2,1)S(1)}, bf16[4,8,2,16,256]{4,3,2,1,0:T(8,128)(2,1)S(1)}, s32[4,8,2,8,128]{4,3,2,1,0:T(8,128)S(1)},...) custom-call(s32[1,24]{1,0:T(1,128)} %bitcast.24, ...), custom_call_target="tpu_custom_call" | custom-call | tf_op jit(solution)/shard_map/gather_blocks/pallas_call | solution.py:200
  39.9 0.0 copy-done
  39.9 103.0 %update_and_exchange.1 = (s16[64,32,896]{2,1,0:T(8,128)(2,1)S(1)}, bf16[288,256]{1,0:T(8,128)(2,1)S(1)}, s32[1,128]{1,0:T(1,128)S(1)}) custom-call(s32[1,128]{1,0:T(1,128)S(1)} %get-tuple-element.19.tile_ref, bf16[64,16,1280]{2,1,0:T(8,128)(2,1)S(1)} %bitcast.13, bf16[64,16,256]{2,1,0:T(8,128)(2,1)S(1)} %bitcast.19, s32[64,8,128]{2,1,0:T(8,128)S(1)} %bitcast.20, ...), custom_call_target="tpu_custom_call" | custom-call | tf_op jit(solution)/shard_map/update_and_exchange/pallas_call | solution.py:444
  142.9 3.2 %place_tiles.1 = (bf16[1,28,32,288]{3,2,1,0:T(8,128)(2,1)}, f32[1,28,32,288]{3,2,1,0:T(8,128)}, f32[1,28,32,288]{3,2,1,0:T(8,128)}, bf16[288,256]{1,0:T(8,128)(2,1)}) custom-call(s32[1,128]{1,0:T(1,128)S(1)} %get-tuple-element.27.from_ref, s16[64,32,896]{2,1,0:T(8,128)(2,1)S(1)} %get-tuple-element.28.inbox_ref, bf16[288,256]{1,0:T(8,128)(2,1)S(1)} %get-tuple-element.29.total_ref), custom_call_target="tpu_custom_call" | custom-call | tf_op jit(solution)/shard_map/place_tiles/pallas_call | solution.py:526
Async XLA Ops:
  0.6 39.2 %copy-start = (bf16[768,288]{0,1:T(8,128)(2,1)S(1)}, bf16[768,288]{0,1:T(8,128)(2,1)}, u32[]{:S(2)}) copy-start(bf16[768,288]{0,1:T(8,128)(2,1)} %param.8) | copy-start | bytes 1327108

commit v5 on v4

--- a/solution.py
+++ b/solution.py
@@ -39,8 +39,8 @@
 KEEP = 1536
 
 
-def gather_kernel(
-    owner_in, slot_in, x_in, c_in, wt_in, onet_in, twot_in,
+def gather_part(
+    owner_smem, owner_in, slot_in, x_in, c_in, wt_in, onet_in, twot_in,
     a_ref, b_ref, t_ref, tile_ref, call_ref, w_ref, one_ref, two_ref,
     owner_ref, slot_ref, x_ref, wt_ref, onet_ref, twot_ref,
     zs, zr, rs, rr, ls, lr, ss, sr, bs, br, bzs, bzr, bss, bsr,
@@ -60,9 +60,17 @@
     partner, x_peers = node_peers_of(n, w)
 
     barrier = pltpu.get_barrier_semaphore()
-    peers = [sibling, partner] + y_peers + z_peers + x_peers
-    for peer in peers:
+    for peer in [partner] + x_peers:
         pl.semaphore_signal(barrier, inc=1, device_id=peer, device_id_type=MESH)
+    many = NZ * NY * NC
+
+    def greet(i, carry):
+        pl.semaphore_signal(
+            barrier, inc=1, device_id=(n, lax.rem(w + i, many)), device_id_type=MESH
+        )
+        return carry
+
+    lax.fori_loop(1, many, greet, 0)
 
     own = [
         pltpu.make_async_copy(src, dst, loc.at[i])
@@ -91,7 +99,7 @@
     t_ref[z, y, c, 1:2, :slot_ref.shape[1]] = slot_ref[...]
     own[1].wait()
 
-    pl.semaphore_wait(barrier, len(peers))
+    pl.semaphore_wait(barrier, many - 1 + NX)
 
     def send(ref, s, r, peer):
         copy = pltpu.make_async_remote_copy(
@@ -151,13 +159,16 @@
             )
         if s == 0:
             sib_b = [send(b_ref.at[z, :, c], bss.at[0], bsr.at[0], sibling)]
-            lane = lax.broadcasted_iota(jnp.int32, tile_ref.shape, 1)
-            tile = jnp.zeros(tile_ref.shape, jnp.int32)
-            for t in range(owner_ref.shape[1]):
-                tile = jnp.where(lane == owner_ref[0:1, t:t + 1], t, tile)
-            tile_ref[...] = tile
+            def tile_at(p, carry):
+                tile = 0
+                for t in range(owner_ref.shape[1]):
+                    tile = jnp.where(owner_smem[0, t] == p, t, tile)
+                tile_ref[p] = tile
+                return carry
+
+            lax.fori_loop(0, many, tile_at, 0)
             own[2].wait()
-            one_ref[...] = onet_ref[...].T
+            one_ref[...] = onet_ref[...].T.reshape(one_ref.shape)
         if s == 1:
             across.wait_recv()
             other = call_ref.at[lax.rem(n + NX, NN)]
@@ -171,10 +182,10 @@
             ]
             sib_t = [send(t_ref.at[z, :, c], tss.at[0], tsr.at[0], sibling)]
             own[3].wait()
-            two_ref[...] = twot_ref[...].T
+            two_ref[...] = twot_ref[...].T.reshape(two_ref.shape)
         if s == 2:
             own[4].wait()
-            w_ref[...] = wt_ref[...].T
+            w_ref[...] = wt_ref[...].T.reshape(w_ref.shape)
     for k in (NZ - 1, 1, 2):
         at = lax.rem(z + k, NZ)
         bz[NZ - k - 1].wait_recv()
@@ -190,69 +201,18 @@
         copy.wait()
 
 
-def gather(owners, slots, features, cotangent, wt, onet, twot):
-    rows, tokens = features.shape
-    cw, ct = cotangent.shape
-    width, depth = wt.shape
-    half = NY // 2
-    pad = rows + rows // 3
-    f32, bf16 = jnp.float32, jnp.bfloat16
-    a, b, t, tile, call, w, one, two = pl.pallas_call(
-        gather_kernel,
-        out_shape=(
-            jax.ShapeDtypeStruct((NZ, NY, NC, pad, HEAD), bf16),
-            jax.ShapeDtypeStruct((NZ, NY, NC, pad, KEEP - HEAD), bf16),
-            jax.ShapeDtypeStruct((NZ, NY, NC, 8, 128), jnp.int32),
-            jax.ShapeDtypeStruct((1, 128), jnp.int32),
-            jax.ShapeDtypeStruct((NN, cw, ct), bf16),
-            jax.ShapeDtypeStruct((depth, width), bf16),
-            jax.ShapeDtypeStruct((depth, width), f32),
-            jax.ShapeDtypeStruct((depth, width), f32),
-        ),
-        in_specs=[HBM] * 7,
-        out_specs=(VMEM,) * 8,
-        scratch_shapes=[
-            pltpu.VMEM(owners.shape, jnp.int32),
-            pltpu.VMEM(slots.shape, jnp.int32),
-            pltpu.VMEM((rows, tokens), bf16),
-            pltpu.VMEM((width, depth), bf16),
-            pltpu.VMEM((width, depth), f32),
-            pltpu.VMEM((width, depth), f32),
-            DMA((NZ - 1,)), DMA((NZ - 1,)),
-            DMA((half, NZ)), DMA((half, NZ)),
-            DMA((half, NZ)), DMA((half, NZ)),
-            DMA((NY + 1,)), DMA((NY + 1,)),
-            DMA((NY - 1,)), DMA((NY - 1,)),
-            DMA((NZ - 1,)), DMA((NZ - 1,)),
-            DMA((NZ,)), DMA((NZ,)),
-            DMA((NY - 1,)), DMA((NY - 1,)),
-            DMA((NZ - 1,)), DMA((NZ - 1,)),
-            DMA((NZ,)), DMA((NZ,)),
-            DMA((NN - 1,)), DMA((NN - 1,)),
-            DMA((7,)),
-        ],
-        compiler_params=pltpu.CompilerParams(
-            collective_id=0, has_side_effects=True, vmem_limit_bytes=32 * 1024 * 1024
-        ),
-        name="gather_blocks",
-    )(*(
-        pltpu.with_memory_space_constraint(v, pltpu.HBM)
-        for v in (owners, slots, features, cotangent, wt, onet, twot)
-    ))
-    many = NZ * NY * NC
-    a, b, t = (v.reshape((many,) + v.shape[3:]) for v in (a, b, t))
-    return a, b, t, tile, call, w, one, two
-
-
 def arrange(a_ref, b_ref, f_ref):
-    blocks, pad, _ = a_ref.shape
+    pad = a_ref.shape[3]
     rows = pad * 3 // 4
     extra = f_ref.shape[1] - KEEP
 
     def four(i, carry):
         at = pl.ds(pl.multiple_of(i * 4 * rows, 16), 4 * rows)
-        a = a_ref[pl.ds(4 * i, 4)]
-        b = b_ref[pl.ds(4 * i, 4)]
+        ys = pl.ds(lax.rem(i, NY // 2) * 2, 2)
+        a = a_ref[i // (NY // 2), ys]
+        b = b_ref[i // (NY // 2), ys]
+        a = a.reshape((4,) + a.shape[2:])
+        b = b.reshape((4,) + b.shape[2:])
         f_ref[at, :HEAD] = jnp.concatenate([a[j, :rows] for j in range(4)], axis=0)
         f_ref[at, HEAD:KEEP] = jnp.concatenate([b[j, :rows] for j in range(4)], axis=0)
         ends = []
@@ -263,7 +223,7 @@
         f_ref[at, KEEP:] = jnp.concatenate(ends, axis=0)
         return carry
 
-    lax.fori_loop(0, blocks // 4, four, 0)
+    lax.fori_loop(0, NZ * NY * NC // 4, four, 0)
 
 
 def fixed_point(x):
@@ -292,7 +252,7 @@
     return jnp.where(code < 0, -v, v)
 
 
-def exchange_kernel(
+def exchange_part(
     tile_ref, a_ref, b_ref, t_ref, c_ref, wt_ref, w_ref, one_ref, two_ref,
     inbox_ref, out_ref, from_ref, f_ref, grad, outbox, share, got, total, across_got,
     send_sem, recv_sem, xs, xr, acs, acr, loc,
@@ -316,17 +276,6 @@
         to_y = lax.rem(y + NY + sign * dy, NY)
         return (to_z * NY + to_y) * NC + lax.rem(c + dc, NC), step
 
-    barrier = pltpu.get_barrier_semaphore()
-    for peer in [partner] + x_peers:
-        pl.semaphore_signal(barrier, inc=1, device_id=peer, device_id_type=MESH)
-
-    def greet(i, carry):
-        p, _ = peer_of(i)
-        pl.semaphore_signal(barrier, inc=1, device_id=(n, p), device_id_type=MESH)
-        return carry
-
-    lax.fori_loop(1, many, greet, 0)
-
     arrange(a_ref, b_ref, f_ref)
     part = grad.shape[0] // 3
     tokens = c_ref.shape[2]
@@ -344,10 +293,9 @@
         return carry
 
     lax.fori_loop(0, 3, multiply, 0)
-    pl.semaphore_wait(barrier, many - 1 + NX)
 
     def pack(p):
-        b = tile_ref[0, p]
+        b = tile_ref[p]
         g = grad[b]
         first = 0.9 * one_ref[b] + 0.1 * g
         second = 0.999 * two_ref[b] + 0.001 * g * g
@@ -404,8 +352,9 @@
 
     blocks = grad.shape[0]
     lane = lax.broadcasted_iota(jnp.int32, (many, 128), 1)
-    ours = jnp.logical_and(t_ref[:, 0, :] == w, lane < blocks)
-    slot = jnp.min(jnp.where(ours, t_ref[:, 1, :], 128), axis=1, keepdims=True)
+    tables = t_ref[...].reshape((many,) + t_ref.shape[3:])
+    ours = jnp.logical_and(tables[:, 0, :] == w, lane < blocks)
+    slot = jnp.min(jnp.where(ours, tables[:, 1, :], 128), axis=1, keepdims=True)
     source = lax.broadcasted_iota(jnp.int32, (many, 128), 0)
     from_ref[...] = jnp.max(jnp.where(slot == lane, source, -1), axis=0, keepdims=True)
 
@@ -433,27 +382,66 @@
         copy.wait_send()
 
 
-def exchange(tile_of, a, b, tables, cots, wt, weight, one, two):
-    depth, width = weight.shape
+def step_kernel(*refs):
+    ins, outs, held, rest = refs[:8], refs[8:11], refs[11:25], refs[25:]
+    (a_ref, b_ref, t_ref, tile_ref, call_ref, w_ref, one_ref, two_ref,
+     owner_ref, slot_ref, x_ref, wt_ref, onet_ref, twot_ref) = held
+    gather_part(*ins, *held, *rest[:23])
+    exchange_part(
+        tile_ref, a_ref, b_ref, t_ref, call_ref, wt_ref, w_ref, one_ref, two_ref,
+        *outs, *rest[23:],
+    )
+
+
+def step(owners, slots, features, cotangent, wt, onet, twot):
+    rows = features.shape[0]
+    width, tokens = cotangent.shape
+    depth = wt.shape[1]
+    half = NY // 2
+    pad = rows + rows // 3
+    peers = NZ * NY * NC
+    blocks = depth // TILE
     lanes = 3 * (width // 128 * 128) + 128
-    blocks = depth // TILE
-    peers = tables.shape[0]
-    tokens = cots.shape[2]
-    f32 = jnp.float32
-    weight, one, two = (v.reshape(blocks, TILE, width) for v in (weight, one, two))
+    i16, i32, f32, bf16 = jnp.int16, jnp.int32, jnp.float32, jnp.bfloat16
     return pl.pallas_call(
-        exchange_kernel,
+        step_kernel,
         out_shape=(
-            jax.ShapeDtypeStruct((peers, TILE, lanes), jnp.int16),
-            jax.ShapeDtypeStruct((width, tokens), jnp.bfloat16),
-            jax.ShapeDtypeStruct((1, 128), jnp.int32),
+            jax.ShapeDtypeStruct((peers, TILE, lanes), i16),
+            jax.ShapeDtypeStruct((width, tokens), bf16),
+            jax.ShapeDtypeStruct((1, 128), i32),
         ),
-        in_specs=[SMEM] + [VMEM] * 8,
-        out_specs=(VMEM, VMEM, VMEM),
+        in_specs=[SMEM] + [HBM] * 7,
+        out_specs=(VMEM,) * 3,
         scratch_shapes=[
-            pltpu.VMEM((depth, tokens * NN), jnp.bfloat16),
+            pltpu.VMEM((NZ, NY, NC, pad, HEAD), bf16),
+            pltpu.VMEM((NZ, NY, NC, pad, KEEP - HEAD), bf16),
+            pltpu.VMEM((NZ, NY, NC, 8, 128), i32),
+            pltpu.SMEM((peers,), i32),
+            pltpu.VMEM((NN, width, tokens), bf16),
+            pltpu.VMEM((blocks, TILE, width), bf16),
             pltpu.VMEM((blocks, TILE, width), f32),
-            pltpu.VMEM((peers, TILE, lanes), jnp.int16),
+            pltpu.VMEM((blocks, TILE, width), f32),
+            pltpu.VMEM(owners.shape, i32),
+            pltpu.VMEM(slots.shape, i32),
+            pltpu.VMEM(features.shape, bf16),
+            pltpu.VMEM((width, depth), bf16),
+            pltpu.VMEM((width, depth), f32),
+            pltpu.VMEM((width, depth), f32),
+            DMA((NZ - 1,)), DMA((NZ - 1,)),
+            DMA((half, NZ)), DMA((half, NZ)),
+            DMA((half, NZ)), DMA((half, NZ)),
+            DMA((NY + 1,)), DMA((NY + 1,)),
+            DMA((NY - 1,)), DMA((NY - 1,)),
+            DMA((NZ - 1,)), DMA((NZ - 1,)),
+            DMA((NZ,)), DMA((NZ,)),
+            DMA((NY - 1,)), DMA((NY - 1,)),
+            DMA((NZ - 1,)), DMA((NZ - 1,)),
+            DMA((NZ,)), DMA((NZ,)),
+            DMA((NN - 1,)), DMA((NN - 1,)),
+            DMA((7,)),
+            pltpu.VMEM((depth, tokens * NN), bf16),
+            pltpu.VMEM((blocks, TILE, width), f32),
+            pltpu.VMEM((peers, TILE, lanes), i16),
             pltpu.VMEM((NX, 2, width, tokens), f32),
             pltpu.VMEM((NX - 1, 2, width, tokens), f32),
             pltpu.VMEM((width, tokens), f32),
@@ -463,10 +451,13 @@
             DMA, DMA, DMA,
         ],
         compiler_params=pltpu.CompilerParams(
-            collective_id=1, has_side_effects=True, vmem_limit_bytes=32 * 1024 * 1024
+            collective_id=0, has_side_effects=True, vmem_limit_bytes=48 * 1024 * 1024
         ),
-        name="update_and_exchange",
-    )(tile_of, a, b, tables, cots, wt, weight, one, two)
+        name="gather_update_exchange",
+    )(owners, *(
+        pltpu.with_memory_space_constraint(v, pltpu.HBM)
+        for v in (owners, slots, features, cotangent, wt, onet, twot)
+    ))
 
 
 PER = 4
@@ -548,11 +539,9 @@
 def on_device(features, weight, moment_one, moment_two, cotangent, new_owner, new_slot):
     blocks = new_owner.shape[2]
     capacity = blocks + blocks // 6
-    wt = weight.T
-    a, b, tables, tile_of, cots, weight_rows, one, two = gather(
-        new_owner[0], new_slot[0], features, cotangent.T, wt, moment_one.T, moment_two.T
+    inbox, total, source = step(
+        new_owner[0], new_slot[0], features, cotangent.T, weight.T, moment_one.T, moment_two.T
     )
-    inbox, total, source = exchange(tile_of, a, b, tables, cots, wt, weight_rows, one, two)
     *moved, projected = place(source, inbox, total, capacity)
     return (projected.T,) + tuple(moved)
 

time: 147 us -> 145 us (0.986)
  Pallas kernels: 145 us -> 142 us
    pallas_call x2 -> x1, Pallas kernels: 142 us -> 139 us  [step(): pl.pallas_call(step_kernel, out_shape=(jax.ShapeDtypeStruct((peers, TILE,...]
where the time goes in v5:
time: 145 us; the launch traced here: 143 us
  Pallas kernels  142 us (98%)
    pallas_call x1, Pallas kernels, step(): pl.pallas_call(step_kernel, out_shape=(jax.ShapeDtypeStruct((peers, TILE,...  139 us
    pallas_call x1, Pallas kernels, place(): pl.pallas_call(place_kernel, out_shape=(pltpu.HBM(shape, bf16), pltpu.HBM...  3.22 us

profile of v5, /device:TPU:1, one launch (start us, length us, event | category | flops | bytes accessed | tf_op | source)
XLA Modules:
  0.0 142.8 jit_solution(3432616213366368920)
XLA Ops:
  0.6 139.0 %gather_update_exchange.1 = (s16[64,32,896]{2,1,0:T(8,128)(2,1)S(1)}, bf16[288,256]{1,0:T(8,128)(2,1)S(1)}, s32[1,128]{1,0:T(1,128)S(1)}) custom-call(s32[1,24]{1,0:T(1,128)} %bitcast.11, s32[1,24]{1,0:T(1,128)} %bitcast.12, s32[1,24]{1,0:T(1,128)} %bitcast.13, bf16[12,2048]{1,0:T(8,128)(2,1)} %refs_3_.1, bf16[288,256]{1,0:T(8,128)(2,1)} %bitcast.10, ...), custom_call_target="tpu_custom_call" | custom-call | tf_op jit(solution)/shard_map/gather_update_exchange/pallas_call | solution.py:406
  139.6 3.2 %place_tiles.1 = (bf16[1,28,32,288]{3,2,1,0:T(8,128)(2,1)}, f32[1,28,32,288]{3,2,1,0:T(8,128)}, f32[1,28,32,288]{3,2,1,0:T(8,128)}, bf16[288,256]{1,0:T(8,128)(2,1)}) custom-call(s32[1,128]{1,0:T(1,128)S(1)} %get-tuple-element.11.from_ref, s16[64,32,896]{2,1,0:T(8,128)(2,1)S(1)} %get-tuple-element.12.inbox_ref, bf16[288,256]{1,0:T(8,128)(2,1)S(1)} %get-tuple-element.13.total_ref), custom_call_target="tpu_custom_call" | custom-call | tf_op jit(solution)/shard_map/place_tiles/pallas_call | solution.py:517

commit v6 on v5

--- a/solution.py
+++ b/solution.py
@@ -269,7 +269,7 @@
     x, high = lax.rem(n, NX), n // NX
 
     def peer_of(i):
-        step = lax.rem(i * 27, many)
+        step = lax.rem(i * 45, many)
         sign = 1 - 2 * c
         dz, dy, dc = place_of(step)
         to_z = lax.rem(z + NZ + sign * dz, NZ)
@@ -282,13 +282,13 @@
 
     def multiply(i, carry):
         at = pl.ds(pl.multiple_of(i * part * TILE, 256), part * TILE)
-        g = jnp.zeros((part * TILE, width), jnp.float32)
+        g = jnp.zeros((width, part * TILE), jnp.float32)
         for k in range(c_ref.shape[0]):
             g += lax.dot_general(
-                f_ref[at, k * tokens:(k + 1) * tokens], c_ref[k],
+                c_ref[k], f_ref[at, k * tokens:(k + 1) * tokens],
                 (((1,), (1,)), ((), ())), preferred_element_type=jnp.float32,
             )
-        g = g.astype(jnp.bfloat16).astype(jnp.float32)
+        g = g.astype(jnp.bfloat16).astype(jnp.float32).T
         grad[pl.ds(i * part, part)] = g.reshape(part, TILE, width)
         return carry
 

time: 145 us -> 141 us (0.972); the launches traced: 143 us -> 141 us
  Pallas kernels: 142 us -> 140 us
    pallas_call x1, Pallas kernels: 139 us -> 137 us  [step(): pl.pallas_call(step_kernel, out_shape=(jax.ShapeDtypeStruct((peers, TILE,...]
where the time goes in v6:
time: 141 us
  Pallas kernels  140 us (99%)
    pallas_call x1, Pallas kernels, step(): pl.pallas_call(step_kernel, out_shape=(jax.ShapeDtypeStruct((peers, TILE,...  137 us
    pallas_call x1, Pallas kernels, place(): pl.pallas_call(place_kernel, out_shape=(pltpu.HBM(shape, bf16), pltpu.HBM...  3.22 us

profile of v6, /device:TPU:1, one launch (start us, length us, event | category | flops | bytes accessed | tf_op | source)
XLA Modules:
  0.0 140.6 jit_solution(14010288789657790715)
XLA Ops:
  0.6 136.8 %gather_update_exchange.1 = (s16[64,32,896]{2,1,0:T(8,128)(2,1)S(1)}, bf16[288,256]{1,0:T(8,128)(2,1)S(1)}, s32[1,128]{1,0:T(1,128)S(1)}) custom-call(s32[1,24]{1,0:T(1,128)} %bitcast.11, s32[1,24]{1,0:T(1,128)} %bitcast.12, s32[1,24]{1,0:T(1,128)} %bitcast.13, bf16[12,2048]{1,0:T(8,128)(2,1)} %refs_3_.1, bf16[288,256]{1,0:T(8,128)(2,1)} %bitcast.10, ...), custom_call_target="tpu_custom_call" | custom-call | tf_op jit(solution)/shard_map/gather_update_exchange/pallas_call | solution.py:406
  137.4 3.2 %place_tiles.1 = (bf16[1,28,32,288]{3,2,1,0:T(8,128)(2,1)}, f32[1,28,32,288]{3,2,1,0:T(8,128)}, f32[1,28,32,288]{3,2,1,0:T(8,128)}, bf16[288,256]{1,0:T(8,128)(2,1)}) custom-call(s32[1,128]{1,0:T(1,128)S(1)} %get-tuple-element.11.from_ref, s16[64,32,896]{2,1,0:T(8,128)(2,1)S(1)} %get-tuple-element.12.inbox_ref, bf16[288,256]{1,0:T(8,128)(2,1)S(1)} %get-tuple-element.13.total_ref), custom_call_target="tpu_custom_call" | custom-call | tf_op jit(solution)/shard_map/place_tiles/pallas_call | solution.py:517

commit v7 on v6

--- a/solution.py
+++ b/solution.py
@@ -223,7 +223,7 @@
         f_ref[at, KEEP:] = jnp.concatenate(ends, axis=0)
         return carry
 
-    lax.fori_loop(0, NZ * NY * NC // 4, four, 0)
+    lax.fori_loop(0, NZ * NY * NC // 4, four, 0, unroll=4)
 
 
 def fixed_point(x):
@@ -292,7 +292,7 @@
         grad[pl.ds(i * part, part)] = g.reshape(part, TILE, width)
         return carry
 
-    lax.fori_loop(0, 3, multiply, 0)
+    lax.fori_loop(0, 3, multiply, 0, unroll=True)
 
     def pack(p):
         b = tile_ref[p]

time: 141 us -> 141 us (level)
  no operation moved by 1% of the time
where the time goes in v7:
time: 141 us; the launch traced here: 140 us
  Pallas kernels  139 us (99%)
    pallas_call x1, Pallas kernels, step(): pl.pallas_call(step_kernel, out_shape=(jax.ShapeDtypeStruct((peers, TILE,...  136 us
    pallas_call x1, Pallas kernels, place(): pl.pallas_call(place_kernel, out_shape=(pltpu.HBM(shape, bf16), pltpu.HBM...  3.22 us

profile of v7, /device:TPU:1, one launch (start us, length us, event | category | flops | bytes accessed | tf_op | source)
XLA Modules:
  0.0 140.1 jit_solution(15511015425934854944)
XLA Ops:
  0.6 136.2 %gather_update_exchange.1 = (s16[64,32,896]{2,1,0:T(8,128)(2,1)S(1)}, bf16[288,256]{1,0:T(8,128)(2,1)S(1)}, s32[1,128]{1,0:T(1,128)S(1)}) custom-call(s32[1,24]{1,0:T(1,128)} %bitcast.11, s32[1,24]{1,0:T(1,128)} %bitcast.12, s32[1,24]{1,0:T(1,128)} %bitcast.13, bf16[12,2048]{1,0:T(8,128)(2,1)} %refs_3_.1, bf16[288,256]{1,0:T(8,128)(2,1)} %bitcast.10, ...), custom_call_target="tpu_custom_call" | custom-call | tf_op jit(solution)/shard_map/gather_update_exchange/pallas_call | solution.py:406
  136.8 3.2 %place_tiles.1 = (bf16[1,28,32,288]{3,2,1,0:T(8,128)(2,1)}, f32[1,28,32,288]{3,2,1,0:T(8,128)}, f32[1,28,32,288]{3,2,1,0:T(8,128)}, bf16[288,256]{1,0:T(8,128)(2,1)}) custom-call(s32[1,128]{1,0:T(1,128)S(1)} %get-tuple-element.11.from_ref, s16[64,32,896]{2,1,0:T(8,128)(2,1)S(1)} %get-tuple-element.12.inbox_ref, bf16[288,256]{1,0:T(8,128)(2,1)S(1)} %get-tuple-element.13.total_ref), custom_call_target="tpu_custom_call" | custom-call | tf_op jit(solution)/shard_map/place_tiles/pallas_call | solution.py:517
